TPU v7x, 256 devices: a whole 4x4x8 slice. The times are simulated.
256 devices in a mesh: ctx: 32 (over y, x, core), head: 8 (over z).
Axes of the slice: x: 4, y: 4, z: 8, core: 2. Of those that a mesh axis runs over, the one named last changes fastest.
Arguments:
- byte_rows: bfloat16 [98304, 2048], P('ctx'), may hold values from -6 to 6
- boundary: int32 [98304], P('ctx'), may hold values from 0 to 1, as said below
- gate_proj: bfloat16 [2048, 4096], P(None, 'head'), may hold values from -0.125 to 0.125
- value_proj: bfloat16 [2048, 4096], P(None, 'head'), may hold values from -0.125 to 0.125
- state_proj: bfloat16 [2048, 256], replicated, may hold values from -0.125 to 0.125
- step_proj: bfloat16 [2048, 64], P(None, 'head'), may hold values from -0.125 to 0.125
- step_bias: float32 [64], P('head'), may hold values from -1 to 0.5
- decay_log: float32 [64], P('head'), may hold values from -12 to -2
- skip_gain: float32 [64], P('head'), may hold values from 0.5 to 1.5
- value_conv: float32 [4, 4096], P(None, 'head'), may hold values from -3 to 3
- value_shift: float32 [4096], P('head'), may hold values from -3 to 3
- state_conv: float32 [4, 256], replicated, may hold values from -3 to 3
- state_shift: float32 [256], replicated, may hold values from -3 to 3
- norm_gain: float32 [4096], P('head'), may hold values from 0.1 to 1.9
Outputs:
- byte_output: float32 [98304, 4096], P('ctx', 'head')
Inputs may be any that keep to these rules, and one draw needn't show every extreme that they name: The first byte is a boundary, and exactly 32768 bytes are boundaries. For every s, the boundaries among bytes s * 3072 to (s + 1) * 3072 - 1 have group numbers from s * 1024 - 512 to (s + 1) * 1024 + 511, and such a range of bytes holds at most 2048 boundaries; in every draw one range reaches both ends of its group numbers and holds 2048 boundaries.
All inputs are finite; a program needn't handle non-finite values.
Results may differ from a plain program's by a relative error of at most 0.008.
Values may be sent and summed in bfloat16 or wider, within the bound.
A program may use at most 128 MiB of HBM per device.

v0:
```python
import jax
import jax.numpy as jnp
from jax import lax
from jax.sharding import PartitionSpec as P

HEAD_DIM = 64
STATE = 128
SSD_BLOCK = 256
GROUP_DEV = 1024
INNER = 4096
DRIFT = 512


EPSILON = 1e-05


def prefix_2(value, axis, join, neutral):
    count, mine = (lax.axis_size(axis), lax.axis_index(axis))
    pieces = jax.tree.map(lambda part: lax.all_gather(part, axis), value)
    running = jax.tree.map(
        lambda part, zero: jnp.full_like(part, 0) + jnp.asarray(zero, part.dtype), value, neutral
    )

    def lap(position, running):
        longer = join(running, jax.tree.map(lambda part: part[position], pieces))
        return jax.tree.map(lambda new, old: jnp.where(position < mine, new, old), longer, running)

    return lax.fori_loop(0, count - 1, lap, running)


def from_behind(array, axis, by):
    count = lax.axis_size(axis)
    pairs = [(i, i + by) for i in range(count) if 0 <= i + by < count]
    return lax.ppermute(array, axis, pairs)


def add_counts(earlier, later):
    return earlier + later


def chain_states(earlier, later):
    return (earlier[0] * later[0], later[0][:, None, None] * earlier[1] + later[1])


def select_rows(byte_rows, byte_of_rank, count, first, length):
    ranks = first + jnp.arange(length, dtype=jnp.int32)
    valid = (ranks >= 0) & (ranks < count)
    sources = jnp.take(byte_of_rank, jnp.clip(ranks, 0, byte_of_rank.shape[0] - 1), axis=0)
    picked = jnp.take(byte_rows, sources, axis=0)
    return jnp.where(valid[:, None], picked, jnp.zeros_like(picked))


def conv_silu(previous, raw, weight, shift):
    length = raw.shape[0]
    extended = jnp.concatenate([previous, raw], 0).astype(jnp.float32)
    total = jnp.zeros((length, raw.shape[1]), jnp.float32) + shift[None, :]
    for kernel_tap in range(weight.shape[0]):
        total = total + weight[kernel_tap][None, :] * extended[kernel_tap : kernel_tap + length]
    return jax.nn.silu(total).astype(jnp.bfloat16)


def shards(
    byte_rows,
    boundary,
    gate_proj,
    value_proj,
    state_proj,
    step_proj,
    step_bias,
    decay_log,
    skip_gain,
    value_conv,
    value_shift,
    state_conv,
    state_shift,
    norm_gain,
):
    bytes_here = boundary.shape[0]
    width = byte_rows.shape[1]
    heads_here = decay_log.shape[0]
    shard = lax.axis_index("ctx")
    local_count = jnp.sum(boundary).reshape(1)
    offsets = prefix_2(local_count, "ctx", add_counts, jnp.zeros((1,), jnp.int32))
    start = offsets[0]
    count = local_count[0]
    local_rank = jnp.cumsum(boundary) - 1
    slots = jnp.where(boundary > 0, local_rank, bytes_here)
    byte_of_rank = (
        jnp.zeros((bytes_here,), jnp.int32)
        .at[slots]
        .set(jnp.arange(bytes_here, dtype=jnp.int32), mode="drop")
    )
    first = shard * GROUP_DEV - start
    own_rows = select_rows(byte_rows, byte_of_rank, count, first, GROUP_DEV)
    right_rows = select_rows(byte_rows, byte_of_rank, count, first + GROUP_DEV, DRIFT)
    left_rows = select_rows(byte_rows, byte_of_rank, count, first - DRIFT, DRIFT)
    from_left = from_behind(right_rows, "ctx", 1)
    from_right = from_behind(left_rows, "ctx", -1)
    middle = jnp.zeros((GROUP_DEV - DRIFT, width), jnp.bfloat16)
    balanced = (
        own_rows
        + jnp.concatenate([from_left, middle], 0)
        + jnp.concatenate([middle, from_right], 0)
    )
    gate = jnp.dot(balanced, gate_proj, preferred_element_type=jnp.float32).astype(jnp.bfloat16)
    value_raw = jnp.dot(balanced, value_proj, preferred_element_type=jnp.float32).astype(
        jnp.bfloat16
    )
    step_raw = jnp.dot(balanced, step_proj, preferred_element_type=jnp.float32).astype(jnp.bfloat16)
    state_raw = jnp.dot(balanced, state_proj, preferred_element_type=jnp.float32).astype(
        jnp.bfloat16
    )
    reach = value_conv.shape[0] - 1
    prior_value, prior_state = from_behind(
        (value_raw[GROUP_DEV - reach :], state_raw[GROUP_DEV - reach :]), "ctx", 1
    )
    values = conv_silu(prior_value, value_raw, value_conv, value_shift)
    states = conv_silu(prior_state, state_raw, state_conv, state_shift)
    steps = jax.nn.softplus(step_raw.astype(jnp.float32) + step_bias[None, :])
    rates = jnp.exp(decay_log)
    block = min(SSD_BLOCK, GROUP_DEV)
    blocks = GROUP_DEV // block
    value_blocks = values.reshape(blocks, block, heads_here, HEAD_DIM)
    in_blocks = states[:, :STATE].reshape(blocks, block, STATE)
    out_blocks = states[:, STATE:].reshape(blocks, block, STATE)
    step_blocks = steps.reshape(blocks, block, heads_here)
    running = jnp.cumsum(-step_blocks * rates[None, None, :], axis=1)
    scores = jnp.einsum("btn,bsn->bts", out_blocks, in_blocks, preferred_element_type=jnp.float32)
    lower = (jnp.arange(block)[:, None] >= jnp.arange(block)[None, :])[None, :, :, None]
    spread = running[:, :, None, :] - running[:, None, :, :]
    weights = jnp.where(
        lower,
        scores[..., None] * jnp.exp(jnp.where(lower, spread, 0.0)) * step_blocks[:, None, :, :],
        0.0,
    )
    weights = weights.astype(jnp.bfloat16)
    intra = jnp.einsum("btsh,bshp->bthp", weights, value_blocks, preferred_element_type=jnp.float32)
    tail = jnp.exp(running[:, -1:, :] - running) * step_blocks
    weighted = value_blocks.astype(jnp.float32) * tail[..., None]
    fresh = jnp.einsum(
        "bshp,bsn->bhpn", weighted, in_blocks.astype(jnp.float32), precision=lax.Precision.HIGHEST
    )
    carried = jnp.zeros((heads_here, HEAD_DIM, STATE), jnp.float32)
    prefix = jnp.zeros((heads_here,), jnp.float32)
    entering = []
    prefixes = []
    for block_index in range(blocks):
        entering.append(carried)
        prefixes.append(prefix)
        carried = jnp.exp(running[block_index, -1])[:, None, None] * carried + fresh[block_index]
        prefix = prefix + running[block_index, -1]
    identity = (
        jnp.ones((heads_here,), jnp.float32),
        jnp.zeros((heads_here, HEAD_DIM, STATE), jnp.float32),
    )
    unused_decay, incoming = prefix_2((jnp.exp(prefix), carried), "ctx", chain_states, identity)
    starting = jnp.stack(entering) + jnp.exp(jnp.stack(prefixes))[:, :, None, None] * incoming[None]
    inter = jnp.exp(running)[..., None] * jnp.einsum(
        "btn,bhpn->bthp", out_blocks.astype(jnp.float32), starting, precision=lax.Precision.HIGHEST
    )
    mixed = intra + inter + skip_gain[None, None, :, None] * value_blocks.astype(jnp.float32)
    gated = mixed.reshape(GROUP_DEV, heads_here * HEAD_DIM) * jax.nn.silu(gate.astype(jnp.float32))
    squares = lax.psum(jnp.sum(gated * gated, axis=1), "head")
    group_out = gated * lax.rsqrt(squares / INNER + EPSILON)[:, None] * norm_gain[None, :]
    from_next = from_behind(group_out[:DRIFT], "ctx", -1)
    from_prev = from_behind(group_out[GROUP_DEV - DRIFT - 1 :], "ctx", 1)
    table = jnp.concatenate([from_prev, group_out, from_next], 0)
    base_place = start - shard * GROUP_DEV + DRIFT + 1
    places = jnp.clip(local_rank + base_place, 0, table.shape[0] - 1)
    return jnp.take(table, places, axis=0)


def solution(mesh):
    placed = (
        P("ctx", None),
        P("ctx"),
        P(None, "head"),
        P(None, "head"),
        P(),
        P(None, "head"),
        P("head"),
        P("head"),
        P("head"),
        P(None, "head"),
        P("head"),
        P(),
        P(),
        P("head"),
    )
    return jax.shard_map(
        shards, mesh=mesh, in_specs=placed, out_specs=P("ctx", "head"), check_vma=False
    )
```

profile of v0, /device:TPU:1, one launch (start us, length us, event | category | flops | bytes accessed | tf_op | source)
XLA Modules:
  0.0 398.9 jit_solution(13126947142720736668)
XLA Ops:
  6.5 1.1 reduce-window.15
  7.9 1.4 fusion.58
  9.3 1.3 dynamic-slice
  10.6 1.3 dynamic-update-slice
  11.9 14.4 %all-reduce.2 = s32[32]{0:T(128)S(1)} all-reduce(s32[32]{0:T(128)S(1)} %dynamic-update-slice), channel_id=1, replica_groups=mesh['ctx'=32,'head'=8] {'ctx'}, use_global_device_ids=true, to_apply=%add.2 | all-reduce | flops 32 | bytes 256
  26.3 37.1 %while.27 = (s32[]{:T(128)}, s32[1]{0:T(128)}, s32[]{:T(128)}, s32[32,1]{0,1:T(1,128)S(1)}, s32[]{:T(128)}) while((s32[]{:T(128)}, s32[1]{0:T(128)}, s32[]{:T(128)}, s32[32,1]{0,1:T(1,128)S(1)}, s32[]{:T(128)}) %tuple.91), condition=%wide.region_4.5_spmd, body=%wide.region_3.4_spmd.sunk | while | flops 5 | bytes 115 | solution.py:28
  64.0 11.8 %scatter_custom_fusion = s32[3072]{0:T(1024)S(1)} fusion(s32[3072]{0:T(1024)S(1)} %get-tuple-element.242, s32[3072]{0:T(1024)S(1)} %iota.39, s32[]{:T(128)} %constant.142.clone.1), kind=kCustom, calls=%fused_computation.101 | custom fusion | bytes 12292 | tf_op jit(solution)/shard_map/scatter | solution.py:91
  75.9 3.1 gather_fusion.5
  79.0 11.4 %gather_fusion.6 = bf16[512,2048]{1,0:T(8,128)(2,1)} fusion(bf16[3072,2048]{1,0:T(8,128)(2,1)} %param.22, s32[1024]{0:T(1024)S(1)} %pad_clamp_fusion), kind=kCustom, calls=%fused_computation.3.clone | custom fusion | bytes 4196352 | tf_op jit(solution)/shard_map/jit(_take)/gather | solution.py:49
  90.5 3.2 select_select_fusion
  93.7 5.9 %collective-permute-start.1 = (bf16[512,2048]{1,0:T(8,128)(2,1)}, bf16[512,2048]{1,0:T(8,128)(2,1)}, u32[]{:S(2)}, u32[]{:S(2)}) collective-permute-start(bf16[512,2048]{1,0:T(8,128)(2,1)} %select_select_fusion), channel_id=1, source_target_pairs={{8,0},{16,8},{24,16},{32,24},{40,32},{48,40},{56,48},{64,56},{72,6... | collective-permute-start | bytes 6291464 | tf_op jit(solution)/shard_map/ppermute | solution.py:34
  100.1 3.1 gather_fusion.3
  103.3 11.4 %gather_fusion.4 = bf16[512,2048]{1,0:T(8,128)(2,1)} fusion(bf16[3072,2048]{1,0:T(8,128)(2,1)} %param.22, s32[1024]{0:T(1024)S(1)} %pad_clamp_fusion.2), kind=kCustom, calls=%fused_computation.1.clone | custom fusion | bytes 4196352 | tf_op jit(solution)/shard_map/jit(_take)/gather | solution.py:49
  114.7 3.3 select_select_fusion.1
  118.0 2.1 collective-permute-start
  120.1 6.2 %gather_fusion = s32[1024]{0:T(1024)S(1)} fusion(s32[3072]{0:T(1024)S(1)} %scatter_custom_fusion, s32[1024]{0:T(1024)S(1)} %broadcast_clamp_fusion.2), kind=kCustom, calls=%fused_computation.4 | custom fusion | bytes 12288 | tf_op jit(solution)/shard_map/jit(_take)/gather | solution.py:48
  126.4 15.0 %gather_fusion.1 = bf16[1024,2048]{1,0:T(8,128)(2,1)} fusion(bf16[3072,2048]{1,0:T(8,128)(2,1)} %param.22, s32[1024]{0:T(1024)S(1)} %broadcast_clamp_fusion.1), kind=kCustom, calls=%fused_computation.5 | custom fusion | bytes 8392704 | tf_op jit(solution)/shard_map/jit(_take)/gather | solution.py:49
  142.1 1.1 collective-permute-done
  143.2 5.6 %pad_add_fusion = bf16[1024,2048]{1,0:T(8,128)(2,1)S(1)} fusion(bf16[512,2048]{1,0:T(8,128)(2,1)} %collective-permute-done.1, bf16[512,2048]{1,0:T(8,128)(2,1)} %collective-permute-done, bf16[1024,2048]{1,0:T(8,128)(2,1)} %gather_fusion.1, pred[1024]{0:T(1024)(128)(4,1)S(1)} %get-tuple-element.254, pred[1024]{0:T(1024)(128)(4,1)S(1)} %get-tuple-element.253), kind=kLoop, calls=%fused_computation.19 | loop fusion | flops 16777216 | bytes 12584960 | tf_op jit(solution)/shard_map/add | solution.py:101
  148.9 1.2 compare_select_fusion
  150.9 2.3 reduce-window.19
  155.1 5.3 %convolution_convert_fusion.1 = bf16[1024,512]{1,0:T(8,128)(2,1)S(1)} fusion(bf16[1024,2048]{1,0:T(8,128)(2,1)} %copy-done.1, bf16[2048,512]{1,0:T(8,128)(2,1)} %param.25), kind=kOutput, calls=%fused_computation.47 | convolution fusion | flops 2148007936 | bytes 7340032 | tf_op jit(solution)/shard_map/dot_general | solution.py:106
  160.5 4.4 %collective-permute-start.2 = (bf16[3,512]{1,0:T(4,128)(2,1)S(1)}, bf16[3,512]{1,0:T(4,128)(2,1)S(1)}, u32[]{:S(2)}, u32[]{:S(2)}) collective-permute-start(bf16[3,512]{1,0:T(4,128)(2,1)S(1)} %slice.161), channel_id=1, source_target_pairs={{0,8},{8,16},{16,24},{24,32},{32,40},{40,48},{48,56},{56,64},{64,7... | collective-permute-start | bytes 9224 | tf_op jit(solution)/shard_map/ppermute | solution.py:34
  164.9 1.2 convolution_convert_fusion.2
  166.1 2.1 collective-permute-start.3
  171.2 1.3 multiply_convert_fusion
  172.5 2.1 reshape.424
  174.7 2.3 copy.42
  177.0 1.2 fusion.8
  178.2 1.1 slice_add_fusion
  181.3 26.9 %all-gather = f32[32,1,8]{2,1,0:T(1,128)} all-gather(f32[1,1,8]{2,1,0:T(1,128)S(1)} %get-tuple-element.232), channel_id=1, replica_groups=mesh['ctx'=32,'head'=8] {'ctx'}, dimensions={0}, use_global_device_ids=true | all-gather | bytes 1056 | tf_op jit(solution)/shard_map/all_gather | solution.py:19
  208.2 1.2 maximum_exponential_fusion
  209.4 2.4 fusion.61
  211.8 29.4 %all-gather.3.cloned.1.call-done = f32[32,8,64,128]{3,2,1,0:T(8,128)} async-done(((f32[1,8,64,128]{3,2,1,0:T(8,128)}), f32[32,8,64,128]{3,2,1,0:T(8,128)}) %all-gather.3.cloned.1.call-update) | async-done | bytes 8388624 | tf_op jit(solution)/shard_map/all_gather | solution.py:19
  241.2 54.4 %while.28 = (s32[]{:T(128)}, f32[8,64,128]{2,1,0:T(8,128)S(1)}, s32[]{:T(128)}, f32[32,8]{1,0:T(8,128)}, f32[32,8,64,128]{3,2,1,0:T(8,128)}, /*index=5*/s32[]{:T(128)}, s32[]{:T(128)}) while((s32[]{:T(128)}, f32[8,64,128]{2,1,0:T(8,128)S(1)}, s32[]{:T(128)}, f32[32,8]{1,0:T(8,128)}, f32[32,8,64,128]{3,2,1,0:T(8,128)}, ...), condition=%wide.region_9.12_spmd.clone, body=%wide.region_8.11_spmd.clone.sunk | while | flops 262148 | bytes 786641 | solution.py:28
  241.9 1.0 fusion.76
  243.7 1.0 fusion.76
  245.4 1.0 fusion.76
  247.2 1.0 fusion.76
  248.9 1.0 fusion.76
  250.7 1.0 fusion.76
  252.5 1.0 fusion.76
  254.2 1.0 fusion.76
  256.0 1.0 fusion.76
  257.7 1.0 fusion.76
  259.5 1.0 fusion.76
  261.2 1.0 fusion.76
  263.0 1.0 fusion.76
  264.7 1.0 fusion.76
  284.0 1.0 fusion.76
  295.7 2.3 fusion.24
  298.0 4.0 %fusion.9 = f32[4,256,8,64]{1,3,2,0:T(8,128)} fusion(bf16[4,256,8,64]{1,3,2,0:T(8,128)(2,1)S(1)} %copy.42, f32[4,256,8,64]{1,3,2,0:T(8,128)S(1)} %fusion.24, f32[4,256,8]{1,2,0:T(8,128)S(1)} %bitcast.113, f32[4,256,8]{1,2,0:T(8,128)S(1)} %get-tuple-element.227, f32[4,256,256]{2,1,0:T(8,128)S(1)} %copy-done.5, pred[256,256]{1,0:T(8,128)(4,1)S(1)} %iota_compare_fusion, ...), kind=kOutput, calls=%fused_computation.27 | convolution fusion | flops 283639808 | bytes 6455328 | tf_op jit(solution)/shard_map/btsh,bshp->bthp/dot_general | solution.py:137
  302.0 3.8 copy.48
  305.8 4.8 %reshape.423 = f32[1024,512]{1,0:T(8,128)} reshape(f32[4,256,8,64]{3,2,1,0:T(8,128)} %copy.48) | data formatting | bytes 4194304 | tf_op jit(solution)/shard_map/reshape | solution.py:162
  310.6 6.9 %multiply_reduce_fusion = (f32[1024]{0:T(1024)S(1)}, f32[1024,512]{1,0:T(8,128)}) fusion(f32[1024,512]{1,0:T(8,128)} %reshape.423, bf16[1024,2048]{1,0:T(8,128)(2,1)} %copy-done.1, bf16[2048,512]{1,0:T(8,128)(2,1)S(1)} %copy-done), kind=kOutput, calls=%fused_computation.44 | convolution fusion | flops 2152201216 | bytes 10489856 | tf_op jit(solution)/shard_map/dot_general | solution.py:105
  317.5 13.8 %psum.7 = f32[1024]{0:T(1024)S(1)} all-reduce(f32[1024]{0:T(1024)S(1)} %get-tuple-element.251), channel_id=1, replica_groups=mesh['ctx'=32,'head'=8] {'head'}, use_global_device_ids=true, to_apply=%region_11.14 | all-reduce | flops 1024 | bytes 8192 | tf_op jit(solution)/shard_map/psum | solution.py:163
  331.4 1.8 multiply_multiply_fusion
  333.5 1.1 copy-done.3
  334.6 6.8 %collective-permute-start.4 = (f32[513,512]{1,0:T(8,128)S(1)}, f32[513,512]{1,0:T(8,128)S(1)}, u32[]{:S(2)}, u32[]{:S(2)}) collective-permute-start(f32[513,512]{1,0:T(8,128)S(1)} %slice.184), channel_id=1, source_target_pairs={{0,8},{8,16},{16,24},{24,32},{32,40},{40,48},{48,56},{56,64},{64,7... | collective-permute-start | bytes 3151880 | tf_op jit(solution)/shard_map/ppermute | solution.py:34
  341.4 1.9 collective-permute-start.5
  343.4 14.0 %collective-permute-done.5 = f32[512,512]{1,0:T(8,128)S(1)} collective-permute-done((f32[512,512]{1,0:T(8,128)S(1)}, f32[512,512]{1,0:T(8,128)S(1)}, u32[]{:S(2)}, u32[]{:S(2)}) %collective-permute-start.5) | collective-permute-done | bytes 1048608 | tf_op jit(solution)/shard_map/ppermute | solution.py:34
  358.5 12.4 %concatenate.23 = f32[2049,512]{1,0:T(8,128)} concatenate(f32[513,512]{1,0:T(8,128)S(1)} %collective-permute-done.4, f32[1024,512]{1,0:T(8,128)} %copy-done.3, f32[512,512]{1,0:T(8,128)} %copy-done.6), dimensions={0} | concatenate | bytes 8392704 | tf_op jit(solution)/shard_map/concatenate | solution.py:167
  370.8 15.9 %gather_fusion.2 = f32[3072,512]{1,0:T(8,128)} fusion(f32[2049,512]{1,0:T(8,128)} %concatenate.23, s32[3072]{0:T(1024)S(1)} %broadcast_clamp_fusion), kind=kCustom, calls=%fused_computation.6 | custom fusion | bytes 12595200 | tf_op jit(solution)/shard_map/jit(_take)/gather | solution.py:170
  386.7 5.4 %broadcast_select_fusion = f32[3072,512]{1,0:T(8,128)} fusion(f32[3072,512]{1,0:T(8,128)} %gather_fusion.2, pred[3072]{0:T(1024)(128)(4,1)S(1)} %compare_and_fusion), kind=kLoop, calls=%fused_computation.21 | loop fusion | flops 1572864 | bytes 12585984 | tf_op jit(solution)/shard_map/jit(_take)/select_n | solution.py:170
  (183 shorter events, 67.4 us)
Async XLA Ops:
  6.5 304.1 %copy-start = (bf16[2048,512]{1,0:T(8,128)(2,1)S(1)}, bf16[2048,512]{1,0:T(8,128)(2,1)}, u32[]{:S(2)}) copy-start(bf16[2048,512]{1,0:T(8,128)(2,1)} %param.24) | copy-start | bytes 6291460
  6.5 234.7 %all-gather.3.cloned.1.call-start = ((), (), s32[]{:S(2)}) async-start(), calls=%async_computation | async-start | bytes 8650752 | tf_op jit(solution)/shard_map/all_gather | solution.py:19
  7.9 172.0 %copy-start.10 = (s32[24]{0:T(128)}, s32[24]{0:T(128)S(1)}, u32[]{:S(2)}) copy-start(s32[24]{0:T(128)S(1)} %slice_reduce_fusion.1) | copy-start | bytes 292
  93.7 48.4 %collective-permute-start.1 = (bf16[512,2048]{1,0:T(8,128)(2,1)}, bf16[512,2048]{1,0:T(8,128)(2,1)}, u32[]{:S(2)}, u32[]{:S(2)}) collective-permute-start(bf16[512,2048]{1,0:T(8,128)(2,1)} %select_select_fusion), channel_id=1, source_target_pairs={{8,0},{16,8},{24,16},{32,24},{40,32},{48,40},{56,48},{64,56},{72,6... | collective-permute-start | bytes 6291464 | tf_op jit(solution)/shard_map/ppermute | solution.py:34
  118.0 25.2 %collective-permute-start = (bf16[512,2048]{1,0:T(8,128)(2,1)}, bf16[512,2048]{1,0:T(8,128)(2,1)}, u32[]{:S(2)}, u32[]{:S(2)}) collective-permute-start(bf16[512,2048]{1,0:T(8,128)(2,1)} %select_select_fusion.1), channel_id=1, source_target_pairs={{0,8},{8,16},{16,24},{24,32},{32,40},{40,48},{48,56},{56,64},{64,7... | collective-permute-start | bytes 6291464 | tf_op jit(solution)/shard_map/ppermute | solution.py:34
  126.3 15.1 %copy-start.23 = (f32[8]{0:T(128)S(1)}, f32[8]{0:T(128)}, u32[]{:S(2)}) copy-start(f32[8]{0:T(128)} %param.29) | copy-start | bytes 100
  126.4 15.6 %copy-start.13 = (f32[4,256]{1,0:T(4,128)S(1)}, f32[4,256]{1,0:T(4,128)}, u32[]{:S(2)}) copy-start(f32[4,256]{1,0:T(4,128)} %param.33) | copy-start | bytes 12292
  126.4 15.7 %copy-start.12 = (f32[4,512]{1,0:T(4,128)S(1)}, f32[4,512]{1,0:T(4,128)}, u32[]{:S(2)}) copy-start(f32[4,512]{1,0:T(4,128)} %param.31) | copy-start | bytes 24580
  143.2 5.6 %copy-start.8 = (bf16[2048,8]{0,1:T(8,128)(2,1)S(1)}, bf16[2048,8]{0,1:T(8,128)(2,1)}, u32[]{:S(2)}) copy-start(bf16[2048,8]{0,1:T(8,128)(2,1)} %param.27) | copy-start | bytes 98308
  143.2 5.6 %copy-start.16 = (f32[8]{0:T(128)S(1)}, f32[8]{0:T(128)}, u32[]{:S(2)}) copy-start(f32[8]{0:T(128)} %param.28) | copy-start | bytes 100
  148.8 2.0 copy-start.1
  155.1 9.8 %copy-start.2 = (bf16[1024,2048]{1,0:T(8,128)(2,1)S(1)}, bf16[1024,2048]{1,0:T(8,128)(2,1)}, u32[]{:S(2)}) copy-start(bf16[1024,2048]{1,0:T(8,128)(2,1)} %copy-done.1) | copy-start | bytes 12582916
  155.1 9.8 %copy-start.22 = (bf16[2048,256]{1,0:T(8,128)(2,1)S(1)}, bf16[2048,256]{1,0:T(8,128)(2,1)}, u32[]{:S(2)}) copy-start(bf16[2048,256]{1,0:T(8,128)(2,1)} %param.26) | copy-start | bytes 3145732
  160.4 8.9 %copy-start.21 = (f32[256]{0:T(256)S(1)}, f32[256]{0:T(256)}, u32[]{:S(2)}) copy-start(f32[256]{0:T(256)} %param.34) | copy-start | bytes 3076
  160.5 10.4 %collective-permute-start.2 = (bf16[3,512]{1,0:T(4,128)(2,1)S(1)}, bf16[3,512]{1,0:T(4,128)(2,1)S(1)}, u32[]{:S(2)}, u32[]{:S(2)}) collective-permute-start(bf16[3,512]{1,0:T(4,128)(2,1)S(1)} %slice.161), channel_id=1, source_target_pairs={{0,8},{8,16},{16,24},{24,32},{32,40},{40,48},{48,56},{56,64},{64,7... | collective-permute-start | bytes 9224 | tf_op jit(solution)/shard_map/ppermute | solution.py:34
  166.1 3.1 collective-permute-start.3
  170.0 1.2 copy-start.14
  174.7 2.3 copy-start.4
  174.7 3.5 copy-start.17
  174.7 3.5 copy-start.18
  174.7 3.5 copy-start.19
  174.7 3.5 copy-start.20
  295.6 2.4 copy-start.5
  295.6 2.4 copy-start.9
  295.6 2.4 copy-start.24
  310.6 20.8 %copy-start.15 = (f32[512]{0:T(512)S(1)}, f32[512]{0:T(512)}, u32[]{:S(2)}) copy-start(f32[512]{0:T(512)} %param.35) | copy-start | bytes 6148
  333.2 1.3 copy-start.3
  333.2 10.1 %copy-start.11 = (s32[24]{0:T(128)S(1)}, s32[24]{0:T(128)}, u32[]{:S(2)}) copy-start(s32[24]{0:T(128)} %copy-done.10) | copy-start | bytes 292
  333.3 10.1 %copy-start.7 = (s32[24,128]{1,0:T(8,128)S(1)}, s32[24,128]{1,0:T(8,128)}, u32[]{:S(2)}) copy-start(s32[24,128]{1,0:T(8,128)} %add_clamp_fusion) | copy-start | bytes 36868
  334.6 23.9 %collective-permute-start.4 = (f32[513,512]{1,0:T(8,128)S(1)}, f32[513,512]{1,0:T(8,128)S(1)}, u32[]{:S(2)}, u32[]{:S(2)}) collective-permute-start(f32[513,512]{1,0:T(8,128)S(1)} %slice.184), channel_id=1, source_target_pairs={{0,8},{8,16},{16,24},{24,32},{32,40},{40,48},{48,56},{56,64},{64,7... | collective-permute-start | bytes 3151880 | tf_op jit(solution)/shard_map/ppermute | solution.py:34
  341.4 16.1 %collective-permute-start.5 = (f32[512,512]{1,0:T(8,128)S(1)}, f32[512,512]{1,0:T(8,128)S(1)}, u32[]{:S(2)}, u32[]{:S(2)}) collective-permute-start(f32[512,512]{1,0:T(8,128)S(1)} %slice.185), channel_id=1, source_target_pairs={{8,0},{16,8},{24,16},{32,24},{40,32},{48,40},{56,48},{64,56},{72,6... | collective-permute-start | bytes 3145736 | tf_op jit(solution)/shard_map/ppermute | solution.py:34
  357.5 1.0 copy-start.6
Sparse Core Ops, SparseCore 0:
  179.4 61.7 all-gather.2
where the time goes:
time: 403 us; the launch traced here: 399 us
  local copies, waits for them, and re-layouts  151 us (37%)
  other arithmetic  66.4 us (16%)
  blocking collectives  55.2 us (14%)
  waiting for transfers between devices  45.4 us (11%)
  matrix products  24.6 us (6%)
  starting transfers between devices  23.2 us (6%)
  loops' own time  19.3 us (5%)
  between operations  14.1 us (3%)
    gather x3, local copies, waits for them, and re-layouts, select_rows(): picked = jnp.take(byte_rows, sources, axis=0)  37.9 us
    select_n x31, other arithmetic, lap(): jnp.where(position < mine, new, old)  32.5 us
    all_gather x1, waiting for transfers between devices, prefix_2(): pieces = jax.tree.map(lambda part: lax.all_gather(part, axis), value)  29.4 us
    all_gather x1, blocking collectives, prefix_2(): pieces = jax.tree.map(lambda part: lax.all_gather(part, axis), value)  26.9 us
    ppermute x6, starting transfers between devices, from_behind(): return lax.ppermute(array, axis, pairs)  23.2 us
    mul x31, local copies, waits for them, and re-layouts, chain_states(): later[0][:, None, None] * earlier[1] + later[1]  21.3 us
    another operation x2, loops' own time, prefix_2(): return lax.fori_loop(0, count - 1, lap, running)  19.3 us
    dynamic_slice x31, local copies, waits for them, and re-layouts, lap(): longer = join(running, jax.tree.map(lambda part: part[position], pieces))  18.3 us
  transfers between devices with their start and end apart: 7, of which 4 were waited for; matrix products, arithmetic and copies ran while one was open for 12% of the time, Pallas kernels for 0%

commit v1 on v0

v1 whole, which is shorter than its diff:
```python
import functools

import jax
import jax.numpy as jnp
from jax import lax
from jax.experimental import pallas as pl
from jax.experimental.pallas import tpu as pltpu
from jax.sharding import PartitionSpec as P

F32 = jnp.float32
BF16 = jnp.bfloat16
I32 = jnp.int32
HEAD_DIM = 64
STATE = 128
HEADS_HERE = 8
WIDE = HEADS_HERE * HEAD_DIM
INNER = 4096
T = 128
BLOCK = 256
SPAN = BLOCK + 16
LEAD = 24
EPSILON = 1e-05
LOG_FLOOR = -1e4
MESH = pl.DeviceIdType.MESH


def on_chip(shape, kind):
    return pltpu.VMEM(shape, kind)


def keep_on_chip(array):
    return pltpu.with_memory_space_constraint(array, pltpu.VMEM)


def keep_off_chip(array):
    return pltpu.with_memory_space_constraint(array, pltpu.HBM)


def dot(a, b):
    return jnp.dot(a, b, preferred_element_type=F32)


def dot_tn(a, b):
    return lax.dot_general(a, b, (((0,), (0,)), ((), ())), preferred_element_type=F32)


def dot_nt(a, b):
    return lax.dot_general(a, b, (((1,), (1,)), ((), ())), preferred_element_type=F32)


def iota(shape, axis):
    return lax.broadcasted_iota(I32, shape, axis)


def silu(v):
    return 0.5 * v * (1.0 + jnp.tanh(0.5 * v))


def flag(condition):
    return jnp.where(condition, 1.0, 0.0).astype(BF16)


def pieces(v, count):
    out = []
    for _ in range(count):
        top = v.astype(BF16).astype(F32)
        out.append(top)
        v = v - top
    return out


def compact_kernel(
    groups,
    bnd_ref,
    bytes_hbm,
    rows_ref,
    tail_ref,
    count_ref,
    rank_ref,
    start_ref,
    held,
    target,
    sems,
):
    blocks = bytes_hbm.shape[0] // BLOCK
    lines = 2 * blocks
    width = rows_ref.shape[1]

    def fetch(j):
        at = pl.ds(pl.multiple_of(j * BLOCK, BLOCK), BLOCK)
        return pltpu.make_async_copy(bytes_hbm.at[at], held.at[at], sems.at[j])

    def begin(j, carry):
        fetch(j).start()
        return carry

    lax.fori_loop(0, blocks, begin, 0)

    bnd = bnd_ref[...].reshape(lines, 128).astype(F32)
    bnd16 = bnd.astype(BF16)
    inside = dot(bnd16, flag(iota((128, 128), 0) <= iota((128, 128), 1)))
    above = dot(flag(iota((lines, lines), 1) < iota((lines, lines), 0)), bnd16)
    before = jnp.sum(above, axis=1, keepdims=True)
    upto = inside + before
    target[...] = jnp.where(bnd > 0, upto - 1.0, -1.0).astype(I32)
    rank_ref[...] = jnp.concatenate([upto, jnp.zeros((128 - lines, 128), F32)], 0).T
    for j in range(blocks):
        start_ref[j] = before[2 * j, 0].astype(I32)
    count = upto[lines - 1, 127].astype(I32)
    count_ref[...] = jnp.full(count_ref.shape, count, I32)
    rows_ref[0:16, :] = jnp.zeros((16, width), BF16)

    def step(j, carry):
        fetch(j).wait()
        base = pl.multiple_of((start_ref[j] // 16) * 16, 16)
        places = iota((SPAN, 128), 0) + base
        left = places == target[pl.ds(2 * j, 1), :]
        right = places == target[pl.ds(2 * j + 1, 1), :]
        choose = jnp.concatenate([flag(left), flag(right)], 1)
        here = pl.ds(pl.multiple_of(j * BLOCK, BLOCK), BLOCK)
        piece = min(512, width)
        for c in range(0, width, piece):
            cols = pl.ds(c, piece)
            picked = dot(choose, held[here, cols]).astype(BF16)
            rows_ref[pl.ds(base, 16), cols] = rows_ref[pl.ds(base, 16), cols] + picked[:16]
            rows_ref[pl.ds(pl.multiple_of(base + 16, 16), BLOCK), cols] = picked[16:]
        return carry

    lax.fori_loop(0, blocks, step, 0)

    clear = (start_ref[blocks - 1] // 16) * 16 + SPAN

    def wipe(i, carry):
        rows_ref[pl.ds(pl.multiple_of(clear + 16 * i, 16), 16), :] = jnp.zeros((16, width), BF16)
        return carry

    lax.fori_loop(0, jnp.maximum(groups + 32 - clear, 0) // 16, wipe, 0)
    near = pl.multiple_of((jnp.maximum(count - 4, 0) // 16) * 16, 16)
    row, column = iota((16, 32), 0), iota((16, 32), 1)
    wanted = count - 16 + row
    choose = flag((row >= 12) & (wanted >= 0) & (column + near == wanted))
    last = dot(choose, rows_ref[pl.ds(near, 32), :])
    few = jnp.minimum(count, 4).astype(F32)
    tail_ref[...] = jnp.where(iota(last.shape, 0) == 0, few, last).astype(BF16)


def compact(boundary, byte_rows, groups):
    length, width = byte_rows.shape
    blocks = length // BLOCK
    vmem = pl.BlockSpec(memory_space=pltpu.VMEM)
    return pl.pallas_call(
        functools.partial(compact_kernel, groups),
        out_shape=[
            on_chip((groups + SPAN, width), BF16),
            on_chip((16, width), BF16),
            on_chip((8, 128), I32),
            on_chip((128, 128), F32),
            jax.ShapeDtypeStruct((blocks,), I32),
        ],
        in_specs=[vmem, pl.BlockSpec(memory_space=pltpu.HBM)],
        out_specs=[vmem, vmem, vmem, vmem, pl.BlockSpec(memory_space=pltpu.SMEM)],
        scratch_shapes=[
            pltpu.VMEM((length, width), BF16),
            pltpu.VMEM((2 * blocks, 128), I32),
            pltpu.SemaphoreType.DMA((blocks,)),
        ],
        compiler_params=pltpu.CompilerParams(vmem_limit_bytes=30 << 20),
        cost_estimate=pl.CostEstimate(
            flops=2 * SPAN * length * width, bytes_accessed=2 * length * width, transcendentals=0
        ),
    )(boundary, byte_rows)


def head_column(ref, shape):
    head = iota(shape, 0) % HEADS_HERE
    out = jnp.zeros(shape, F32)
    for h in range(HEADS_HERE):
        out = jnp.where(head == h, ref[h], out)
    return out


def layer_kernel(
    n_ctx,
    n_head,
    groups,
    rows_ref,
    tail_ref,
    count_ref,
    value_ref,
    gate_ref,
    state_ref,
    step_ref,
    bias_ref,
    log_ref,
    skip_ref,
    vconv_ref,
    vshift_ref,
    sconv_ref,
    sshift_ref,
    table_ref,
    inv_ref,
    ext,
    xs,
    maps,
    mix,
    open_gate,
    grow,
    fresh,
    raw_step,
    lead_t,
    lead_e,
    minus,
    sel_d,
    sel_e,
    near,
    halo_gate,
    out_slices,
    in_slices,
    ret_out,
    ret_in,
    entry,
    squares,
    near_send,
    near_recv,
    out_send,
    out_recv,
    ret_send,
    ret_recv,
    sq_send,
    sq_recv,
):
    me = lax.axis_index("ctx")
    column = lax.axis_index("head")
    subs = groups // T
    share = STATE * 4 // n_ctx
    big = 2 * T
    bigs = groups // big

    barrier = pltpu.get_barrier_semaphore()

    def greet_ctx(d, carry):
        pl.semaphore_signal(
            barrier, inc=1, device_id={"ctx": lax.rem(me + d, n_ctx)}, device_id_type=MESH
        )
        return carry

    def greet_head(d, carry):
        pl.semaphore_signal(
            barrier, inc=1, device_id={"head": lax.rem(column + d, n_head)}, device_id_type=MESH
        )
        return carry

    lax.fori_loop(1, n_ctx, greet_ctx, 0)
    lax.fori_loop(1, n_head, greet_head, 0)
    pl.semaphore_wait(barrier, n_ctx - 1 + n_head - 1)

    def near_copy(d):
        return pltpu.make_async_remote_copy(
            src_ref=tail_ref,
            dst_ref=near.at[d - 1],
            send_sem=near_send.at[d - 1],
            recv_sem=near_recv.at[d - 1],
            device_id={"ctx": lax.rem(me + d, n_ctx)},
            device_id_type=MESH,
        )

    near_copy(1).start()
    near_copy(2).start()

    for i in range(groups // 512):
        got = dot_nt(step_ref[...], rows_ref[i * 512 : (i + 1) * 512, :])
        for q in range(4):
            k = i * 4 + q
            raw_step[k * 8 : (k + 1) * 8, :] = got[:8, q * T : (q + 1) * T]
    shape = (subs * 8, T)
    raw = raw_step[...] + head_column(bias_ref, shape)
    soft = jnp.maximum(raw, 0.0) + jnp.log1p(jnp.exp(-jnp.abs(raw)))
    valid = (iota(shape, 0) // 8) * T + iota(shape, 1) < count_ref[0:1, :]
    step = jnp.where(valid, soft, 0.0)
    logs = jnp.where(valid, jnp.maximum(jnp.log(soft), LOG_FLOOR), LOG_FLOOR)
    decay = -step * jnp.exp(head_column(log_ref, shape))
    tri = flag(iota((T, T), 0) <= iota((T, T), 1))
    d0, d1, d2 = pieces(decay, 3)
    cum = (dot(d0.astype(BF16), tri) + dot(d1.astype(BF16), tri)) + dot(d2.astype(BF16), tri)
    total = jnp.broadcast_to(cum[:, T - 1 : T], shape)
    cums = pieces(cum, 3)
    lows = pieces(logs - cum, 3)
    grows = pieces(jnp.exp(cum), 2)
    tails = pieces(jnp.exp(total - cum) * step, 2)
    for k in range(subs):
        at = slice(k * 8, (k + 1) * 8)
        lead_t[k] = jnp.concatenate([p[at] for p in cums] + [jnp.ones((24, T), F32)], 0).astype(BF16)
        lead_e[k] = jnp.concatenate([p[at] for p in grows + tails], 0).astype(BF16)
        minus[k] = jnp.concatenate([p[at] for p in lows], 0)
    head_of = iota((24, 8 * T), 0) % 8
    sel_d[...] = flag(head_of == iota((24, 8 * T), 1) // T).astype(F32)
    row, lane = iota((32, 2 * WIDE), 0), iota((32, 2 * WIDE), 1)
    sel_e[...] = flag((row % 8 == (lane % WIDE) // HEAD_DIM) & ((row < 16) == (lane < WIDE)))

    near_copy(1).wait()
    near_copy(2).wait()
    first = jnp.where(me >= 1, near[0].astype(F32), 0.0)
    second = jnp.where(me >= 2, near[1].astype(F32), 0.0)
    few = jnp.broadcast_to(near[0][0:1, 0:16].astype(F32), (16, 16))
    few = jnp.where(me >= 1, few, 4.0)
    row, lane = iota((16, 16), 0), iota((16, 16), 1)
    shift = flag((row >= 12) & (lane >= 12) & (lane.astype(F32) == row.astype(F32) + few))
    halo = dot(shift, second.astype(BF16)) + jnp.where(iota(first.shape, 0) >= 12, first, 0.0)
    halo = halo.astype(BF16)
    ext[0 : LEAD - 16, :] = jnp.zeros((LEAD - 16, ext.shape[1]), F32)
    ext[LEAD - 16 : LEAD, :WIDE] = dot(halo, value_ref[...])
    ext[LEAD - 16 : LEAD, WIDE:] = dot(halo, state_ref[...])
    halo_gate[...] = silu(dot(halo, gate_ref[...]))

    def convolve(at, length):
        seen = ext[pl.ds(at, length + 8), :]
        for taps, shifts, lo, hi in (
            (vconv_ref, vshift_ref, 0, WIDE),
            (sconv_ref, sshift_ref, WIDE, WIDE + 2 * STATE),
        ):
            sum_ = shifts[...] + taps[0:1, :] * seen[5 : 5 + length, lo:hi]
            for j in range(1, 4):
                sum_ = sum_ + taps[j : j + 1, :] * seen[5 + j : 5 + j + length, lo:hi]
            yield silu(sum_).astype(BF16)

    x_h, m_h = convolve(0, 16)

    def local(i, carry):
        state, product = carry
        g0 = pl.multiple_of(i * big, big)
        here = pl.ds(g0, big)
        ext[pl.ds(g0 + LEAD, big), :WIDE] = dot(rows_ref[here, :], value_ref[...])
        ext[pl.ds(g0 + LEAD, big), WIDE:] = dot(rows_ref[here, :], state_ref[...])
        x, m = convolve(g0 + LEAD - 8, big)
        xs[here, :] = x
        maps[here, :] = m
        for q in range(big // T):
            k = i * (big // T) + q
            at = slice(q * T, (q + 1) * T)
            both = dot_tn(lead_e[k], sel_e[...])
            grow[k] = both[:, :WIDE]
            weighted = (x[at].astype(F32) * both[:, WIDE:]).astype(BF16)
            new = dot_tn(m[at, :STATE], weighted)
            fresh[k] = new
            factor = both[T - 1 : T, :WIDE]
            state = factor * state + new
            product = factor * product
        return state, product

    state, product = lax.fori_loop(
        0, bigs, local, (jnp.zeros((STATE, WIDE), F32), jnp.ones((1, WIDE), F32))
    )

    high, low = pieces(jnp.broadcast_to(product, (8, WIDE)), 2)
    ends = jnp.concatenate([high, low], 0).astype(BF16)
    whole = state.astype(BF16)
    for k in range(n_ctx):
        r, c = (k // 4) * share, (k % 4) * 128
        out_slices[k, :share, :] = whole[r : r + share, c : c + 128]
        out_slices[k, share:, :] = ends[:, c : c + 128]

    def out_copy(d):
        to = lax.rem(me + d, n_ctx)
        return pltpu.make_async_remote_copy(
            src_ref=out_slices.at[to],
            dst_ref=in_slices.at[me],
            send_sem=out_send.at[d],
            recv_sem=out_recv.at[d],
            device_id={"ctx": to},
            device_id_type=MESH,
        )

    def ret_copy(d):
        to = lax.rem(me + d, n_ctx)
        return pltpu.make_async_remote_copy(
            src_ref=ret_out.at[to],
            dst_ref=ret_in.at[me],
            send_sem=ret_send.at[d],
            recv_sem=ret_recv.at[d],
            device_id={"ctx": to},
            device_id_type=MESH,
        )

    def start_all(copy, count):
        lax.fori_loop(1, count, lambda d, c: (copy(d).start(), c)[1], 0)

    def wait_all(copy, count):
        lax.fori_loop(1, count, lambda d, c: (copy(d).wait(), c)[1], 0)

    in_slices[me] = out_slices[me]
    start_all(out_copy, n_ctx)

    skip = jnp.zeros((1, WIDE), F32)
    for h in range(HEADS_HERE):
        skip = jnp.where(iota((1, WIDE), 1) // HEAD_DIM == h, skip_ref[h], skip)
    lower = iota((T, T), 1) <= iota((T, T), 0)
    left_half = iota((T, T), 1) < HEAD_DIM

    def inside(i, carry):
        g0 = pl.multiple_of(i * big, big)
        here = pl.ds(g0, big)
        open_gate[here, :] = silu(dot(rows_ref[here, :], gate_ref[...]))
        for q in range(big // T):
            k = i * (big // T) + q
            at = pl.ds(pl.multiple_of(g0 + q * T, T), T)
            x, m = xs[at, :], maps[at, :]
            scores = jnp.where(lower, dot_nt(m[:, STATE:], m[:, :STATE]), 0.0)
            lows = minus[k]
            tile = jnp.concatenate([lows] * HEADS_HERE, 1) * sel_d[...]
            right = jnp.concatenate([sel_d[...], tile], 0).astype(BF16)
            spread = dot_tn(lead_t[k], right)
            weight = jnp.exp(jnp.minimum(spread, 60.0))
            weight = (weight * jnp.concatenate([scores] * HEADS_HERE, 1)).astype(BF16)
            for p in range(HEADS_HERE // 2):
                pair = x[:, p * T : (p + 1) * T]
                stacked = jnp.concatenate(
                    [
                        jnp.where(left_half, pair, jnp.zeros_like(pair)),
                        jnp.where(left_half, jnp.zeros_like(pair), pair),
                    ],
                    0,
                )
                got = dot(weight[:, 2 * p * T : 2 * (p + 1) * T], stacked)
                cols = slice(p * T, (p + 1) * T)
                mix[at, cols] = got + skip[:, cols] * pair.astype(F32)
        return carry

    half = bigs // 2
    lax.fori_loop(0, half, inside, 0)

    wait_all(out_copy, n_ctx)
    running = jnp.zeros((share, 128), F32)
    for i in range(n_ctx):
        ret_out[i] = running.astype(BF16)
        got = in_slices[i].astype(F32)
        factor = got[share : share + 1] + got[share + 8 : share + 9]
        running = factor * running + got[:share]
    ret_in[me] = ret_out[me]
    start_all(ret_copy, n_ctx)

    lax.fori_loop(half, bigs, inside, 0)

    wait_all(ret_copy, n_ctx)
    for k in range(n_ctx):
        r, c = (k // 4) * share, (k % 4) * 128
        entry[r : r + share, c : c + 128] = ret_in[k]

    ones = jnp.ones((8, WIDE), BF16)
    y_h = dot(m_h[:, STATE:], entry[...]) + skip * x_h.astype(F32)
    g_h = y_h * halo_gate[...]
    table_ref[0 : T - 16, :] = jnp.zeros((T - 16, WIDE), BF16)
    table_ref[T - 16 : T, :] = g_h.astype(BF16)
    power = jnp.concatenate([jnp.zeros((T - 16, WIDE), F32), g_h * g_h], 0).astype(BF16)
    mine = squares.at[column]
    mine[...] = jnp.zeros(mine.shape, F32)
    mine[0:1, :] = dot_nt(ones, power)[0:1, :]

    def outer(k, state):
        at = pl.ds(pl.multiple_of(k * T, T), T)
        factor = grow[k]
        inter = dot(maps[at, STATE:], state.astype(BF16))
        gated = (mix[at, :] + factor * inter) * open_gate[at, :]
        table_ref[pl.ds(pl.multiple_of((k + 1) * T, T), T), :] = gated.astype(BF16)
        squares[column, pl.ds(k + 1, 1), :] = dot_nt(ones, (gated * gated).astype(BF16))[0:1, :]
        return factor[T - 1 : T, :] * state + fresh[k]

    lax.fori_loop(0, subs, outer, entry[...].astype(F32))

    def sq_copy(d):
        return pltpu.make_async_remote_copy(
            src_ref=squares.at[column],
            dst_ref=squares.at[column],
            send_sem=sq_send.at[d],
            recv_sem=sq_recv.at[d],
            device_id={"head": lax.rem(column + d, n_head)},
            device_id_type=MESH,
        )

    start_all(sq_copy, n_head)
    wait_all(sq_copy, n_head)
    power = squares[0]
    for i in range(1, n_head):
        power = power + squares[i]
    inv_ref[...] = lax.rsqrt(power * (1.0 / (n_head * WIDE)) + EPSILON)


def layer(n_ctx, n_head, groups, *args):
    subs = groups // T
    share = STATE * 4 // n_ctx
    lines = -(-(subs + 1) // 8) * 8
    vmem = pl.BlockSpec(memory_space=pltpu.VMEM)
    smem = pl.BlockSpec(memory_space=pltpu.SMEM)
    width = args[0].shape[1]
    sem = pltpu.SemaphoreType.DMA
    return pl.pallas_call(
        functools.partial(layer_kernel, n_ctx, n_head, groups),
        out_shape=[
            on_chip((groups + T, WIDE), BF16),
            on_chip((lines, T), F32),
        ],
        in_specs=[vmem] * 7 + [smem] * 3 + [vmem] * 4,
        out_specs=[vmem, vmem],
        scratch_shapes=[
            pltpu.VMEM((groups + LEAD, WIDE + 2 * STATE), F32),
            pltpu.VMEM((groups, WIDE), BF16),
            pltpu.VMEM((groups, 2 * STATE), BF16),
            pltpu.VMEM((groups, WIDE), F32),
            pltpu.VMEM((groups, WIDE), F32),
            pltpu.VMEM((subs, T, WIDE), F32),
            pltpu.VMEM((subs, STATE, WIDE), F32),
            pltpu.VMEM((subs * 8, T), F32),
            pltpu.VMEM((subs, 48, T), BF16),
            pltpu.VMEM((subs, 32, T), BF16),
            pltpu.VMEM((subs, 24, T), F32),
            pltpu.VMEM((24, 8 * T), F32),
            pltpu.VMEM((32, 2 * WIDE), BF16),
            pltpu.VMEM((2, 16, width), BF16),
            pltpu.VMEM((16, WIDE), F32),
            pltpu.VMEM((n_ctx, share + 16, 128), BF16),
            pltpu.VMEM((n_ctx, share + 16, 128), BF16),
            pltpu.VMEM((n_ctx, share, 128), BF16),
            pltpu.VMEM((n_ctx, share, 128), BF16),
            pltpu.VMEM((STATE, WIDE), BF16),
            pltpu.VMEM((n_head, lines, T), F32),
            sem((2,)),
            sem((2,)),
            sem((n_ctx,)),
            sem((n_ctx,)),
            sem((n_ctx,)),
            sem((n_ctx,)),
            sem((n_head,)),
            sem((n_head,)),
        ],
        compiler_params=pltpu.CompilerParams(
            collective_id=0, has_side_effects=True, vmem_limit_bytes=32 << 20
        ),
        cost_estimate=pl.CostEstimate(
            flops=2 * groups * width * 1536, bytes_accessed=8 << 20, transcendentals=1 << 22
        ),
    )(*args)


def expand_kernel(
    groups, start_ref, rank_ref, table_ref, inv_ref, gain_ref, out_hbm, ready, sems
):
    blocks = out_hbm.shape[0] // BLOCK
    window = min(3 * T, groups + T)

    def send(j):
        at = pl.ds(pl.multiple_of(j * BLOCK, BLOCK), BLOCK)
        return pltpu.make_async_copy(ready.at[at], out_hbm.at[at], sems.at[j])

    def step(j, carry):
        line = jnp.minimum((start_ref[j] + T - 1) // T, (groups + T - window) // T)
        base = pl.multiple_of(line * T, T)
        lane = iota((T, T), 1)
        places, scales = [], []
        for half in range(2):
            rank = jnp.sum(
                jnp.where(lane == 2 * j + half, rank_ref[...], 0.0), axis=1, keepdims=True
            )
            place = jnp.broadcast_to(rank.astype(I32) + (T - 1) - base, (T, T))
            hits = [place == lane + w * T for w in range(window // T)]
            places.append(jnp.concatenate([flag(hit) for hit in hits], 1))
            scale = jnp.zeros((T, T), F32)
            for w, hit in enumerate(hits):
                scale = jnp.where(hit, inv_ref[pl.ds(line + w, 1), :], scale)
            scales.append(jnp.sum(scale, axis=1, keepdims=True))
        got = dot(jnp.concatenate(places, 0), table_ref[pl.ds(base, window), :])
        got = got * gain_ref[...] * jnp.concatenate(scales, 0)
        ready[pl.ds(pl.multiple_of(j * BLOCK, BLOCK), BLOCK), :] = got
        send(j).start()
        return carry

    lax.fori_loop(0, blocks, step, 0)

    def finish(j, carry):
        send(j).wait()
        return carry

    lax.fori_loop(0, blocks, finish, 0)


def expand(length, groups, starts, rank, table, inv, gain):
    vmem = pl.BlockSpec(memory_space=pltpu.VMEM)
    return pl.pallas_call(
        functools.partial(expand_kernel, groups),
        out_shape=jax.ShapeDtypeStruct((length, WIDE), F32),
        in_specs=[pl.BlockSpec(memory_space=pltpu.SMEM), vmem, vmem, vmem, vmem],
        out_specs=pl.BlockSpec(memory_space=pl.ANY),
        scratch_shapes=[
            pltpu.VMEM((length, WIDE), F32),
            pltpu.SemaphoreType.DMA((length // BLOCK,)),
        ],
        compiler_params=pltpu.CompilerParams(vmem_limit_bytes=24 << 20),
        cost_estimate=pl.CostEstimate(
            flops=2 * length * 3 * T * WIDE, bytes_accessed=4 * length * WIDE, transcendentals=0
        ),
    )(starts, rank, table, inv, gain)


def shards(
    groups,
    byte_rows,
    boundary,
    gate_proj,
    value_proj,
    state_proj,
    step_proj,
    step_bias,
    decay_log,
    skip_gain,
    value_conv,
    value_shift,
    state_conv,
    state_shift,
    norm_gain,
):
    n_ctx, n_head = lax.axis_size("ctx"), lax.axis_size("head")
    step_t = jnp.concatenate([step_proj.T, jnp.zeros_like(step_proj.T)], 0)
    weights = [keep_on_chip(w) for w in (value_proj, gate_proj, state_proj)]
    rows, tail, count, rank, starts = compact(boundary, keep_off_chip(byte_rows), groups)
    table, inv = layer(
        n_ctx,
        n_head,
        groups,
        rows,
        tail,
        count,
        *weights,
        step_t,
        step_bias,
        decay_log,
        skip_gain,
        value_conv,
        value_shift.reshape(1, -1),
        state_conv,
        state_shift.reshape(1, -1),
    )
    return expand(byte_rows.shape[0], groups, starts, rank, table, inv, norm_gain.reshape(1, -1))


def solution(mesh, groups=2048):
    placed = (
        P("ctx", None),
        P("ctx"),
        P(None, "head"),
        P(None, "head"),
        P(),
        P(None, "head"),
        P("head"),
        P("head"),
        P("head"),
        P(None, "head"),
        P("head"),
        P(),
        P(),
        P("head"),
    )
    return jax.shard_map(
        functools.partial(shards, groups),
        mesh=mesh,
        in_specs=placed,
        out_specs=P("ctx", "head"),
        check_vma=False,
    )
```

time: 403 us -> 74.2 us (0.18)
  local copies, waits for them, and re-layouts: 151 us -> 1.53 us
  Pallas kernels: 0 us -> 72.3 us
  other arithmetic: 66.4 us -> 0 us
  blocking collectives: 55.2 us -> 0 us
  waiting for transfers between devices: 45.4 us -> 0 us
  matrix products: 24.6 us -> 0 us
  starting transfers between devices: 23.2 us -> 0 us
  loops' own time: 19.3 us -> 0 us
  between operations: 14.1 us -> 0.17 us
    pallas_call x0 -> x3, Pallas kernels: none -> 72.3 us  [the longest x1 58.3 us: layer(): pl.pallas_call(functools.partial(layer_kernel, n_ctx, n_head, groups), ou...]
    gather x7 -> x0, local copies, waits for them, and re-layouts: 66.2 us -> none  [the longest x3 37.9 us: select_rows(): picked = jnp.take(byte_rows, sources, axis=0)]
    select_n x39 -> x0, other arithmetic: 44.4 us -> none  [the longest x31 32.5 us: lap(): jnp.where(position < mine, new, old)]
    all_gather x1 -> x0, waiting for transfers between devices: 29.4 us -> none  [prefix_2(): pieces = jax.tree.map(lambda part: lax.all_gather(part, axis), value)]
    all_gather x1 -> x0, blocking collectives: 26.9 us -> none  [prefix_2(): pieces = jax.tree.map(lambda part: lax.all_gather(part, axis), value)]
    dot_general x8 -> x0, matrix products: 24.6 us -> none  [the longest x1 6.89 us: shards(): jnp.dot(balanced, gate_proj, preferred_element_type=jnp.float32)]
    ppermute x6 -> x0, starting transfers between devices: 23.2 us -> none  [from_behind(): return lax.ppermute(array, axis, pairs)]
    mul x31 -> x0, local copies, waits for them, and re-layouts: 21.3 us -> none  [chain_states(): later[0][:, None, None] * earlier[1] + later[1]]
  transfers between devices with their start and end apart: 7 -> 0, of which waited for: 4 -> 0; matrix products, arithmetic and copies ran while one was open for 12% -> 0% of each run, Pallas kernels for 0% -> 0%
where the time goes in v1:
time: 74.2 us; the launch traced here: 74 us
  Pallas kernels  72.3 us (97%)
  local copies, waits for them, and re-layouts  1.53 us (2%)
    pallas_call x1, Pallas kernels, layer(): pl.pallas_call(functools.partial(layer_kernel, n_ctx, n_head, groups), ou...  58.3 us
    pallas_call x1, Pallas kernels, compact(): pl.pallas_call(functools.partial(compact_kernel, groups), out_shape=[on_c...  7.98 us
    pallas_call x1, Pallas kernels, expand(): pl.pallas_call(functools.partial(expand_kernel, groups), out_shape=jax.Sh...  6.02 us

profile of v1, /device:TPU:1, one launch (start us, length us, event | category | flops | bytes accessed | tf_op | source)
XLA Modules:
  0.0 74.0 jit_solution(9325960905367033312)
XLA Ops:
  0.0 0.8 %concatenate.3.step_ref = bf16[16,2048]{1,0:T(8,128)(2,1)S(1)} pad(bf16[8,2048]{1,0:T(8,128)(2,1)} %bitcast.7, bf16[]{:T(256)} %constant.0.clone.1), padding=0_8x0_0 | pad | bytes 98306 | tf_op jit(solution)/shard_map/concatenate | solution.py:620
  0.8 0.0 copy-start.4
  0.8 0.7 copy-done.4
  1.5 0.0 copy-start.1
  1.5 0.0 copy-start.2
  1.5 0.0 copy-start.3
  1.5 0.0 copy-start.5
  1.5 0.0 copy-start.6
  1.5 0.0 copy-start.7
  1.5 0.0 copy-start.8
  1.5 0.0 copy-start.9
  1.5 0.0 copy-start.10
  1.5 0.0 copy-start.11
  1.6 8.0 %shard_map.136 = (bf16[2320,2048]{1,0:T(8,128)(2,1)S(1)}, bf16[16,2048]{1,0:T(8,128)(2,1)S(1)}, s32[8,128]{1,0:T(8,128)S(1)}, f32[128,128]{1,0:T(8,128)S(1)}, s32[12]{0:T(128)S(1)}) custom-call(s32[3072]{0:T(1024)S(1)} %copy-done.4, bf16[3072,2048]{1,0:T(8,128)(2,1)} %bytes_hbm.1), custom_call_target="tpu_custom_call" | custom-call | flops 3422552064 | bytes 12582912 | tf_op jit(solution)/shard_map/pallas_call | solution.py:151
  9.5 0.0 copy-done.1
  9.6 0.0 copy-done.2
  9.6 0.0 copy-done.3
  9.6 0.0 copy-done.5
  9.6 0.0 copy-done.6
  9.6 0.0 copy-done.7
  9.6 0.0 copy-done.8
  9.6 0.0 copy-done.9
  9.6 0.0 copy-done.10
  9.6 0.0 copy-done.11
  9.6 0.0 copy-start
  9.7 58.3 %shard_map.137 = (bf16[2176,512]{1,0:T(8,128)(2,1)S(1)}, f32[24,128]{1,0:T(8,128)S(1)}) custom-call(bf16[2320,2048]{1,0:T(8,128)(2,1)S(1)} %get-tuple-element.14.rows_ref, bf16[16,2048]{1,0:T(8,128)(2,1)S(1)} %get-tuple-element.15.tail_ref, s32[8,128]{1,0:T(8,128)S(1)} %get-tuple-element.16.count_ref, bf16[2048,512]{1,0:T(8,128)(2,1)S(1)} %copy-done.1, ...), custom_call_target="tpu_custom_call" | custom-call | flops 12884901888 | bytes 8388608 | tf_op jit(solution)/shard_map/pallas_call | solution.py:495
  68.0 0.0 copy-done
  68.0 6.0 %shard_map.138 = f32[3072,512]{1,0:T(8,128)} custom-call(s32[12]{0:T(128)S(1)} %get-tuple-element.12.start_ref, f32[128,128]{1,0:T(8,128)S(1)} %get-tuple-element.13.rank_ref, bf16[2176,512]{1,0:T(8,128)(2,1)S(1)} %get-tuple-element.17.table_ref, f32[24,128]{1,0:T(8,128)S(1)} %get-tuple-element.18.inv_ref, f32[1,512]{1,0:T(1,128)S(1)} %bitcast.4), custom_call_target="tpu_custom_call" | custom-call | flops 1207959552 | bytes 6291456 | tf_op jit(solution)/shard_map/pallas_call | solution.py:586
Async XLA Ops:
  0.8 0.7 copy-start.4
  1.5 8.1 %copy-start.1 = (bf16[2048,512]{1,0:T(8,128)(2,1)S(1)}, bf16[2048,512]{1,0:T(8,128)(2,1)}, u32[]{:S(2)}) copy-start(bf16[2048,512]{1,0:T(8,128)(2,1)} %value_ref.1) | copy-start | bytes 6291460
  1.5 8.1 %copy-start.2 = (bf16[2048,512]{1,0:T(8,128)(2,1)S(1)}, bf16[2048,512]{1,0:T(8,128)(2,1)}, u32[]{:S(2)}) copy-start(bf16[2048,512]{1,0:T(8,128)(2,1)} %gate_ref.1) | copy-start | bytes 6291460
  1.5 8.1 %copy-start.3 = (bf16[2048,256]{1,0:T(8,128)(2,1)S(1)}, bf16[2048,256]{1,0:T(8,128)(2,1)}, u32[]{:S(2)}) copy-start(bf16[2048,256]{1,0:T(8,128)(2,1)} %state_ref.1) | copy-start | bytes 3145732
  1.5 8.1 %copy-start.5 = (f32[4,512]{1,0:T(4,128)S(1)}, f32[4,512]{1,0:T(4,128)}, u32[]{:S(2)}) copy-start(f32[4,512]{1,0:T(4,128)} %vconv_ref.1) | copy-start | bytes 24580
  1.5 8.1 %copy-start.6 = (f32[4,256]{1,0:T(4,128)S(1)}, f32[4,256]{1,0:T(4,128)}, u32[]{:S(2)}) copy-start(f32[4,256]{1,0:T(4,128)} %sconv_ref.1) | copy-start | bytes 12292
  1.5 8.1 %copy-start.7 = (f32[512]{0:T(512)S(1)}, f32[512]{0:T(512)}, u32[]{:S(2)}) copy-start(f32[512]{0:T(512)} %param.24) | copy-start | bytes 6148
  1.5 8.1 %copy-start.8 = (f32[256]{0:T(256)S(1)}, f32[256]{0:T(256)}, u32[]{:S(2)}) copy-start(f32[256]{0:T(256)} %param.26) | copy-start | bytes 3076
  1.5 8.1 %copy-start.9 = (f32[8]{0:T(128)S(1)}, f32[8]{0:T(128)}, u32[]{:S(2)}) copy-start(f32[8]{0:T(128)} %bias_ref.1) | copy-start | bytes 100
  1.5 8.1 %copy-start.10 = (f32[8]{0:T(128)S(1)}, f32[8]{0:T(128)}, u32[]{:S(2)}) copy-start(f32[8]{0:T(128)} %log_ref.1) | copy-start | bytes 100
  1.5 8.1 %copy-start.11 = (f32[8]{0:T(128)S(1)}, f32[8]{0:T(128)}, u32[]{:S(2)}) copy-start(f32[8]{0:T(128)} %skip_ref.1) | copy-start | bytes 100
  9.6 58.3 %copy-start = (f32[512]{0:T(512)S(1)}, f32[512]{0:T(512)}, u32[]{:S(2)}) copy-start(f32[512]{0:T(512)} %param.27) | copy-start | bytes 6148

commit v2 on v1

--- a/solution.py
+++ b/solution.py
@@ -18,7 +18,7 @@
 T = 128
 BLOCK = 256
 SPAN = BLOCK + 16
-LEAD = 24
+UNROLL = 3
 EPSILON = 1e-05
 LOG_FLOOR = -1e4
 MESH = pl.DeviceIdType.MESH
@@ -71,7 +71,7 @@
 
 def compact_kernel(
     groups,
-    bnd_ref,
+    bnd_hbm,
     bytes_hbm,
     rows_ref,
     tail_ref,
@@ -80,7 +80,9 @@
     start_ref,
     held,
     target,
+    bnd_ref,
     sems,
+    bnd_sem,
 ):
     blocks = bytes_hbm.shape[0] // BLOCK
     lines = 2 * blocks
@@ -94,7 +96,10 @@
         fetch(j).start()
         return carry
 
+    flags = pltpu.make_async_copy(bnd_hbm, bnd_ref, bnd_sem)
+    flags.start()
     lax.fori_loop(0, blocks, begin, 0)
+    flags.wait()
 
     bnd = bnd_ref[...].reshape(lines, 128).astype(F32)
     bnd16 = bnd.astype(BF16)
@@ -157,12 +162,14 @@
             on_chip((128, 128), F32),
             jax.ShapeDtypeStruct((blocks,), I32),
         ],
-        in_specs=[vmem, pl.BlockSpec(memory_space=pltpu.HBM)],
+        in_specs=[pl.BlockSpec(memory_space=pltpu.HBM)] * 2,
         out_specs=[vmem, vmem, vmem, vmem, pl.BlockSpec(memory_space=pltpu.SMEM)],
         scratch_shapes=[
             pltpu.VMEM((length, width), BF16),
             pltpu.VMEM((2 * blocks, 128), I32),
+            pltpu.VMEM((length,), I32),
             pltpu.SemaphoreType.DMA((blocks,)),
+            pltpu.SemaphoreType.DMA,
         ],
         compiler_params=pltpu.CompilerParams(vmem_limit_bytes=30 << 20),
         cost_estimate=pl.CostEstimate(
@@ -190,22 +197,26 @@
     gate_ref,
     state_ref,
     step_ref,
-    bias_ref,
-    log_ref,
-    skip_ref,
     vconv_ref,
     vshift_ref,
     sconv_ref,
     sshift_ref,
-    table_ref,
+    bias_ref,
+    log_ref,
+    skip_ref,
+    table,
     inv_ref,
-    ext,
+    ext_a,
+    ext_b,
+    ext_h,
+    taps,
     xs,
     maps,
     mix,
     open_gate,
     grow,
-    fresh,
+    locs,
+    fades,
     raw_step,
     lead_t,
     lead_e,
@@ -214,6 +225,8 @@
     sel_e,
     near,
     halo_gate,
+    ends_out,
+    ends_in,
     out_slices,
     in_slices,
     ret_out,
@@ -222,6 +235,8 @@
     squares,
     near_send,
     near_recv,
+    end_send,
+    end_recv,
     out_send,
     out_recv,
     ret_send,
@@ -252,7 +267,6 @@
 
     lax.fori_loop(1, n_ctx, greet_ctx, 0)
     lax.fori_loop(1, n_head, greet_head, 0)
-    pl.semaphore_wait(barrier, n_ctx - 1 + n_head - 1)
 
     def near_copy(d):
         return pltpu.make_async_remote_copy(
@@ -264,14 +278,65 @@
             device_id_type=MESH,
         )
 
-    near_copy(1).start()
-    near_copy(2).start()
+    def end_copy(d):
+        to = lax.rem(me + d, n_ctx)
+        return pltpu.make_async_remote_copy(
+            src_ref=ends_out.at[lax.rem(to, 4)],
+            dst_ref=ends_in.at[me],
+            send_sem=end_send.at[d],
+            recv_sem=end_recv.at[d],
+            device_id={"ctx": to},
+            device_id_type=MESH,
+        )
+
+    def out_copy(d):
+        to = lax.rem(me + d, n_ctx)
+        return pltpu.make_async_remote_copy(
+            src_ref=out_slices.at[to],
+            dst_ref=in_slices.at[me],
+            send_sem=out_send.at[d],
+            recv_sem=out_recv.at[d],
+            device_id={"ctx": to},
+            device_id_type=MESH,
+        )
+
+    def ret_copy(d):
+        to = lax.rem(me + d, n_ctx)
+        return pltpu.make_async_remote_copy(
+            src_ref=ret_out.at[to],
+            dst_ref=ret_in.at[me],
+            send_sem=ret_send.at[d],
+            recv_sem=ret_recv.at[d],
+            device_id={"ctx": to},
+            device_id_type=MESH,
+        )
+
+    def sq_copy(d):
+        return pltpu.make_async_remote_copy(
+            src_ref=squares.at[column],
+            dst_ref=squares.at[column],
+            send_sem=sq_send.at[d],
+            recv_sem=sq_recv.at[d],
+            device_id={"head": lax.rem(column + d, n_head)},
+            device_id_type=MESH,
+        )
+
+    def start_all(copy, count):
+        lax.fori_loop(1, count, lambda d, c: (copy(d).start(), c)[1], 0)
+
+    def wait_all(copy, count):
+        lax.fori_loop(1, count, lambda d, c: (copy(d).wait(), c)[1], 0)
 
     for i in range(groups // 512):
         got = dot_nt(step_ref[...], rows_ref[i * 512 : (i + 1) * 512, :])
         for q in range(4):
             k = i * 4 + q
-            raw_step[k * 8 : (k + 1) * 8, :] = got[:8, q * T : (q + 1) * T]
+            raw_step[k * 8 : (k + 1) * 8, :] = got[:, q * T : (q + 1) * T]
+
+    pl.semaphore_wait(barrier, n_ctx - 1 + n_head - 1)
+    near_copy(1).start()
+    near_copy(2).start()
+
     shape = (subs * 8, T)
     raw = raw_step[...] + head_column(bias_ref, shape)
     soft = jnp.maximum(raw, 0.0) + jnp.log1p(jnp.exp(-jnp.abs(raw)))
@@ -287,6 +352,25 @@
     lows = pieces(logs - cum, 3)
     grows = pieces(jnp.exp(cum), 2)
     tails = pieces(jnp.exp(total - cum) * step, 2)
+
+    over = total[0:8]
+    for k in range(1, subs):
+        over = over + total[k * 8 : (k + 1) * 8]
+    high, low = pieces(jnp.exp(over), 2)
+    first_half = iota((8, T), 1) < HEAD_DIM
+    for c in range(4):
+        both = [
+            jnp.where(
+                first_half,
+                jnp.broadcast_to(part[2 * c : 2 * c + 1], (8, T)),
+                jnp.broadcast_to(part[2 * c + 1 : 2 * c + 2], (8, T)),
+            )
+            for part in (high, low)
+        ]
+        ends_out[c] = jnp.concatenate(both, 0).astype(BF16)
+    ends_in[me] = ends_out[lax.rem(me, 4)]
+    start_all(end_copy, n_ctx)
+
     for k in range(subs):
         at = slice(k * 8, (k + 1) * 8)
         lead_t[k] = jnp.concatenate([p[at] for p in cums] + [jnp.ones((24, T), F32)], 0).astype(BF16)
@@ -296,6 +380,32 @@
     sel_d[...] = flag(head_of == iota((24, 8 * T), 1) // T).astype(F32)
     row, lane = iota((32, 2 * WIDE), 0), iota((32, 2 * WIDE), 1)
     sel_e[...] = flag((row % 8 == (lane % WIDE) // HEAD_DIM) & ((row < 16) == (lane < WIDE)))
+    for c in range(6):
+        tap, move, at = (
+            (vconv_ref, vshift_ref, slice(c * 128, (c + 1) * 128))
+            if c < 4
+            else (sconv_ref, sshift_ref, slice((c - 4) * 128, (c - 3) * 128))
+        )
+        taps[c, 0:4, :] = 0.5 * tap[:, at]
+        taps[c, 4:5, :] = 0.5 * move[:, at]
+
+    def weights_of(n):
+        return value_ref[:, n * 256 : (n + 1) * 256] if n < 2 else state_ref[...]
+
+    def project(block, ext, n):
+        here = pl.ds(pl.multiple_of(block * big, big), big)
+        got = dot(rows_ref[here, :], weights_of(n))
+        ext[2 * n, 8 : 8 + big, :] = got[:, :128]
+        ext[2 * n + 1, 8 : 8 + big, :] = got[:, 128:]
+
+    def convolve(ext, c, at, length):
+        h = taps[c, 4:5, :] + taps[c, 0:1, :] * ext[c, at + 5 : at + 5 + length, :]
+        for j in range(1, 4):
+            h = h + taps[c, j : j + 1, :] * ext[c, at + 5 + j : at + 5 + j + length, :]
+        return h + h * jnp.tanh(h)
+
+    for n in range(3):
+        project(0, ext_a, n)
 
     near_copy(1).wait()
     near_copy(2).wait()
@@ -307,86 +417,62 @@
     shift = flag((row >= 12) & (lane >= 12) & (lane.astype(F32) == row.astype(F32) + few))
     halo = dot(shift, second.astype(BF16)) + jnp.where(iota(first.shape, 0) >= 12, first, 0.0)
     halo = halo.astype(BF16)
-    ext[0 : LEAD - 16, :] = jnp.zeros((LEAD - 16, ext.shape[1]), F32)
-    ext[LEAD - 16 : LEAD, :WIDE] = dot(halo, value_ref[...])
-    ext[LEAD - 16 : LEAD, WIDE:] = dot(halo, state_ref[...])
+    for n in range(3):
+        got = dot(halo, weights_of(n))
+        ext_h[2 * n, 8:24, :] = got[:, :128]
+        ext_h[2 * n + 1, 8:24, :] = got[:, 128:]
     halo_gate[...] = silu(dot(halo, gate_ref[...]))
-
-    def convolve(at, length):
-        seen = ext[pl.ds(at, length + 8), :]
-        for taps, shifts, lo, hi in (
-            (vconv_ref, vshift_ref, 0, WIDE),
-            (sconv_ref, sshift_ref, WIDE, WIDE + 2 * STATE),
-        ):
-            sum_ = shifts[...] + taps[0:1, :] * seen[5 : 5 + length, lo:hi]
-            for j in range(1, 4):
-                sum_ = sum_ + taps[j : j + 1, :] * seen[5 + j : 5 + j + length, lo:hi]
-            yield silu(sum_).astype(BF16)
-
-    x_h, m_h = convolve(0, 16)
-
-    def local(i, carry):
-        state, product = carry
-        g0 = pl.multiple_of(i * big, big)
-        here = pl.ds(g0, big)
-        ext[pl.ds(g0 + LEAD, big), :WIDE] = dot(rows_ref[here, :], value_ref[...])
-        ext[pl.ds(g0 + LEAD, big), WIDE:] = dot(rows_ref[here, :], state_ref[...])
-        x, m = convolve(g0 + LEAD - 8, big)
-        xs[here, :] = x
-        maps[here, :] = m
-        for q in range(big // T):
-            k = i * (big // T) + q
-            at = slice(q * T, (q + 1) * T)
+    for c in range(6):
+        ext_h[c, 0:8, :] = jnp.zeros((8, 128), F32)
+        ext_a[c, 0:8, :] = ext_h[c, 16:24, :]
+    x_h = jnp.concatenate([convolve(ext_h, c, 0, 16) for c in range(4)], 1)
+    c_h = convolve(ext_h, 5, 0, 16).astype(BF16)
+
+    locs[0] = jnp.zeros((STATE, WIDE), F32)
+    fades[0] = jnp.ones((1, WIDE), F32)
+
+    def advance(block, ext, onto, target):
+        for q in range(2):
+            k = block * 2 + q
+            at = pl.ds(pl.multiple_of(k * T, T), T)
+            if target is not None:
+                project(target, onto, 2 * q)
+                if q == 0:
+                    project(target, onto, 1)
             both = dot_tn(lead_e[k], sel_e[...])
             grow[k] = both[:, :WIDE]
-            weighted = (x[at].astype(F32) * both[:, WIDE:]).astype(BF16)
-            new = dot_tn(m[at, :STATE], weighted)
-            fresh[k] = new
+            weighted = []
+            for c in range(4):
+                x = convolve(ext, c, q * T, T)
+                xs[at, c * 128 : (c + 1) * 128] = x.astype(BF16)
+                tail = both[:, WIDE + c * 128 : WIDE + (c + 1) * 128]
+                weighted.append((x * tail).astype(BF16))
+            for c in range(2):
+                maps[at, c * 128 : (c + 1) * 128] = convolve(ext, 4 + c, q * T, T).astype(BF16)
+            new = dot_tn(maps[at, :STATE], jnp.concatenate(weighted, 1))
             factor = both[T - 1 : T, :WIDE]
-            state = factor * state + new
-            product = factor * product
-        return state, product
-
-    state, product = lax.fori_loop(
-        0, bigs, local, (jnp.zeros((STATE, WIDE), F32), jnp.ones((1, WIDE), F32))
-    )
-
-    high, low = pieces(jnp.broadcast_to(product, (8, WIDE)), 2)
-    ends = jnp.concatenate([high, low], 0).astype(BF16)
-    whole = state.astype(BF16)
+            locs[k + 1] = factor * locs[k] + new
+            fades[k + 1] = factor * fades[k]
+
+    def hand_on(source, ext):
+        for c in range(6):
+            ext[c, 0:8, :] = source[c, big : big + 8, :]
+
+    def local(j, carry):
+        advance(2 * j, ext_a, ext_b, 2 * j + 1)
+        hand_on(ext_a, ext_b)
+        advance(2 * j + 1, ext_b, ext_a, 2 * j + 2)
+        hand_on(ext_b, ext_a)
+        return carry
+
+    lax.fori_loop(0, bigs // 2 - 1, local, 0)
+    advance(bigs - 2, ext_a, ext_b, bigs - 1)
+    hand_on(ext_a, ext_b)
+    advance(bigs - 1, ext_b, None, None)
+
     for k in range(n_ctx):
         r, c = (k // 4) * share, (k % 4) * 128
-        out_slices[k, :share, :] = whole[r : r + share, c : c + 128]
-        out_slices[k, share:, :] = ends[:, c : c + 128]
-
-    def out_copy(d):
-        to = lax.rem(me + d, n_ctx)
-        return pltpu.make_async_remote_copy(
-            src_ref=out_slices.at[to],
-            dst_ref=in_slices.at[me],
-            send_sem=out_send.at[d],
-            recv_sem=out_recv.at[d],
-            device_id={"ctx": to},
-            device_id_type=MESH,
-        )
-
-    def ret_copy(d):
-        to = lax.rem(me + d, n_ctx)
-        return pltpu.make_async_remote_copy(
-            src_ref=ret_out.at[to],
-            dst_ref=ret_in.at[me],
-            send_sem=ret_send.at[d],
-            recv_sem=ret_recv.at[d],
-            device_id={"ctx": to},
-            device_id_type=MESH,
-        )
-
-    def start_all(copy, count):
-        lax.fori_loop(1, count, lambda d, c: (copy(d).start(), c)[1], 0)
-
-    def wait_all(copy, count):
-        lax.fori_loop(1, count, lambda d, c: (copy(d).wait(), c)[1], 0)
-
+        out_slices[k] = locs[subs, r : r + share, c : c + 128].astype(BF16)
     in_slices[me] = out_slices[me]
     start_all(out_copy, n_ctx)
 
@@ -428,13 +514,14 @@
     half = bigs // 2
     lax.fori_loop(0, half, inside, 0)
 
+    wait_all(end_copy, n_ctx)
     wait_all(out_copy, n_ctx)
     running = jnp.zeros((share, 128), F32)
     for i in range(n_ctx):
         ret_out[i] = running.astype(BF16)
-        got = in_slices[i].astype(F32)
-        factor = got[share : share + 1] + got[share + 8 : share + 9]
-        running = factor * running + got[:share]
+        factor = ends_in[i].astype(F32)
+        factor = factor[0:1] + factor[8:9]
+        running = factor * running + in_slices[i].astype(F32)
     ret_in[me] = ret_out[me]
     start_all(ret_copy, n_ctx)
 
@@ -446,37 +533,30 @@
         entry[r : r + share, c : c + 128] = ret_in[k]
 
     ones = jnp.ones((8, WIDE), BF16)
-    y_h = dot(m_h[:, STATE:], entry[...]) + skip * x_h.astype(F32)
+    y_h = dot(c_h, entry[...]) + skip * x_h
     g_h = y_h * halo_gate[...]
-    table_ref[0 : T - 16, :] = jnp.zeros((T - 16, WIDE), BF16)
-    table_ref[T - 16 : T, :] = g_h.astype(BF16)
+    table[0 : T - 16, :] = jnp.zeros((T - 16, WIDE), BF16)
+    table[T - 16 : T, :] = g_h.astype(BF16)
     power = jnp.concatenate([jnp.zeros((T - 16, WIDE), F32), g_h * g_h], 0).astype(BF16)
     mine = squares.at[column]
     mine[...] = jnp.zeros(mine.shape, F32)
     mine[0:1, :] = dot_nt(ones, power)[0:1, :]
-
-    def outer(k, state):
-        at = pl.ds(pl.multiple_of(k * T, T), T)
-        factor = grow[k]
-        inter = dot(maps[at, STATE:], state.astype(BF16))
-        gated = (mix[at, :] + factor * inter) * open_gate[at, :]
-        table_ref[pl.ds(pl.multiple_of((k + 1) * T, T), T), :] = gated.astype(BF16)
-        squares[column, pl.ds(k + 1, 1), :] = dot_nt(ones, (gated * gated).astype(BF16))[0:1, :]
-        return factor[T - 1 : T, :] * state + fresh[k]
-
-    lax.fori_loop(0, subs, outer, entry[...].astype(F32))
-
-    def sq_copy(d):
-        return pltpu.make_async_remote_copy(
-            src_ref=squares.at[column],
-            dst_ref=squares.at[column],
-            send_sem=sq_send.at[d],
-            recv_sem=sq_recv.at[d],
-            device_id={"head": lax.rem(column + d, n_head)},
-            device_id_type=MESH,
-        )
-
+    entering = entry[...].astype(F32)
+
+    def outer(i, carry):
+        for q in range(4):
+            k = i * 4 + q
+            at = pl.ds(pl.multiple_of(k * T, T), T)
+            state = (locs[k] + fades[k] * entering).astype(BF16)
+            gated = mix[at, :] + grow[k] * dot(maps[at, STATE:], state)
+            gated = gated * open_gate[at, :]
+            table[pl.ds(pl.multiple_of((k + 1) * T, T), T), :] = gated.astype(BF16)
+            squares[column, pl.ds(k + 1, 1), :] = dot_nt(ones, (gated * gated).astype(BF16))[0:1, :]
+        return carry
+
+    lax.fori_loop(0, subs // 4, outer, 0)
     start_all(sq_copy, n_head)
+
     wait_all(sq_copy, n_head)
     power = squares[0]
     for i in range(1, n_head):
@@ -494,20 +574,21 @@
     sem = pltpu.SemaphoreType.DMA
     return pl.pallas_call(
         functools.partial(layer_kernel, n_ctx, n_head, groups),
-        out_shape=[
-            on_chip((groups + T, WIDE), BF16),
-            on_chip((lines, T), F32),
-        ],
-        in_specs=[vmem] * 7 + [smem] * 3 + [vmem] * 4,
+        out_shape=[on_chip((groups + T, WIDE), BF16), on_chip((lines, T), F32)],
+        in_specs=[vmem] * 11 + [smem] * 3,
         out_specs=[vmem, vmem],
         scratch_shapes=[
-            pltpu.VMEM((groups + LEAD, WIDE + 2 * STATE), F32),
+            pltpu.VMEM((6, 2 * T + 8, 128), F32),
+            pltpu.VMEM((6, 2 * T + 8, 128), F32),
+            pltpu.VMEM((6, 24, 128), F32),
+            pltpu.VMEM((6, 8, 128), F32),
             pltpu.VMEM((groups, WIDE), BF16),
             pltpu.VMEM((groups, 2 * STATE), BF16),
             pltpu.VMEM((groups, WIDE), F32),
             pltpu.VMEM((groups, WIDE), F32),
             pltpu.VMEM((subs, T, WIDE), F32),
-            pltpu.VMEM((subs, STATE, WIDE), F32),
+            pltpu.VMEM((subs + 1, STATE, WIDE), F32),
+            pltpu.VMEM((subs + 1, 1, WIDE), F32),
             pltpu.VMEM((subs * 8, T), F32),
             pltpu.VMEM((subs, 48, T), BF16),
             pltpu.VMEM((subs, 32, T), BF16),
@@ -516,14 +597,18 @@
             pltpu.VMEM((32, 2 * WIDE), BF16),
             pltpu.VMEM((2, 16, width), BF16),
             pltpu.VMEM((16, WIDE), F32),
-            pltpu.VMEM((n_ctx, share + 16, 128), BF16),
-            pltpu.VMEM((n_ctx, share + 16, 128), BF16),
+            pltpu.VMEM((4, 16, 128), BF16),
+            pltpu.VMEM((n_ctx, 16, 128), BF16),
+            pltpu.VMEM((n_ctx, share, 128), BF16),
+            pltpu.VMEM((n_ctx, share, 128), BF16),
             pltpu.VMEM((n_ctx, share, 128), BF16),
             pltpu.VMEM((n_ctx, share, 128), BF16),
             pltpu.VMEM((STATE, WIDE), BF16),
             pltpu.VMEM((n_head, lines, T), F32),
             sem((2,)),
             sem((2,)),
+            sem((n_ctx,)),
+            sem((n_ctx,)),
             sem((n_ctx,)),
             sem((n_ctx,)),
             sem((n_ctx,)),
@@ -572,7 +657,12 @@
         send(j).start()
         return carry
 
-    lax.fori_loop(0, blocks, step, 0)
+    def steps(i, carry):
+        for q in range(UNROLL):
+            step(i * UNROLL + q, 0)
+        return carry
+
+    lax.fori_loop(0, blocks // UNROLL, steps, 0)
 
     def finish(j, carry):
         send(j).wait()
@@ -617,9 +707,10 @@
     norm_gain,
 ):
     n_ctx, n_head = lax.axis_size("ctx"), lax.axis_size("head")
-    step_t = jnp.concatenate([step_proj.T, jnp.zeros_like(step_proj.T)], 0)
-    weights = [keep_on_chip(w) for w in (value_proj, gate_proj, state_proj)]
-    rows, tail, count, rank, starts = compact(boundary, keep_off_chip(byte_rows), groups)
+    weights = [keep_on_chip(w) for w in (value_proj, gate_proj, state_proj, step_proj.T)]
+    rows, tail, count, rank, starts = compact(
+        keep_off_chip(boundary), keep_off_chip(byte_rows), groups
+    )
     table, inv = layer(
         n_ctx,
         n_head,
@@ -628,14 +719,13 @@
         tail,
         count,
         *weights,
-        step_t,
-        step_bias,
-        decay_log,
-        skip_gain,
         value_conv,
         value_shift.reshape(1, -1),
         state_conv,
         state_shift.reshape(1, -1),
+        step_bias,
+        decay_log,
+        skip_gain,
     )
     return expand(byte_rows.shape[0], groups, starts, rank, table, inv, norm_gain.reshape(1, -1))
 

time: 74.2 us -> 61.8 us (0.83)
  Pallas kernels: 72.3 us -> 61.1 us
  local copies, waits for them, and re-layouts: 1.53 us -> 0.05 us
    pallas_call x1, Pallas kernels: 58.3 us -> 48.2 us  [layer(): pl.pallas_call(functools.partial(layer_kernel, n_ctx, n_head, groups), ou...]
    pallas_call x1, Pallas kernels: 6.02 us -> 4.54 us  [expand(): pl.pallas_call(functools.partial(expand_kernel, groups), out_shape=jax.Sh...]
    concatenate x1 -> x0, local copies, waits for them, and re-layouts: 0.76 us -> none  [shards(): step_t = jnp.concatenate([step_proj.T, jnp.zeros_like(step_proj.T)], 0)]
where the time goes in v2:
time: 61.8 us; the launch traced here: 61.3 us
  Pallas kernels  61.1 us (99%)
    pallas_call x1, Pallas kernels, layer(): pl.pallas_call(functools.partial(layer_kernel, n_ctx, n_head, groups), ou...  48.2 us
    pallas_call x1, Pallas kernels, compact(): pl.pallas_call(functools.partial(compact_kernel, groups), out_shape=[on_c...  8.36 us
    pallas_call x1, Pallas kernels, expand(): pl.pallas_call(functools.partial(expand_kernel, groups), out_shape=jax.Sh...  4.54 us

profile of v2, /device:TPU:1, one launch (start us, length us, event | category | flops | bytes accessed | tf_op | source)
XLA Modules:
  0.0 61.3 jit_solution(2219530364960403239)
XLA Ops:
  0.0 0.0 copy-start.1
  0.0 0.0 copy-start.2
  0.0 0.0 copy-start.3
  0.0 0.0 copy-start.4
  0.0 0.0 copy-start.5
  0.0 0.0 copy-start.6
  0.0 0.0 copy-start.7
  0.0 0.0 copy-start.8
  0.1 0.0 copy-start.9
  0.1 0.0 copy-start.10
  0.1 0.0 copy-start.11
  0.1 8.4 %shard_map.136 = (bf16[2320,2048]{1,0:T(8,128)(2,1)S(1)}, bf16[16,2048]{1,0:T(8,128)(2,1)S(1)}, s32[8,128]{1,0:T(8,128)S(1)}, f32[128,128]{1,0:T(8,128)S(1)}, s32[12]{0:T(128)S(1)}) custom-call(s32[3072]{0:T(1024)} %bnd_hbm.1, bf16[3072,2048]{1,0:T(8,128)(2,1)} %bytes_hbm.1), custom_call_target="tpu_custom_call" | custom-call | flops 3422552064 | bytes 12582912 | tf_op jit(solution)/shard_map/pallas_call | solution.py:156
  8.5 0.0 copy-done.1
  8.5 0.0 copy-done.2
  8.5 0.0 copy-done.3
  8.5 0.0 copy-done.4
  8.5 0.0 copy-done.5
  8.5 0.0 copy-done.6
  8.5 0.0 copy-done.7
  8.5 0.0 copy-done.8
  8.5 0.0 copy-done.9
  8.5 0.0 copy-done.10
  8.6 0.0 copy-done.11
  8.6 0.0 copy-start
  8.6 48.2 %shard_map.137 = (bf16[2176,512]{1,0:T(8,128)(2,1)S(1)}, f32[24,128]{1,0:T(8,128)S(1)}) custom-call(bf16[2320,2048]{1,0:T(8,128)(2,1)S(1)} %get-tuple-element.14.rows_ref, bf16[16,2048]{1,0:T(8,128)(2,1)S(1)} %get-tuple-element.15.tail_ref, s32[8,128]{1,0:T(8,128)S(1)} %get-tuple-element.16.count_ref, bf16[2048,512]{1,0:T(8,128)(2,1)S(1)} %copy-done.1, ...), custom_call_target="tpu_custom_call" | custom-call | flops 12884901888 | bytes 8388608 | tf_op jit(solution)/shard_map/pallas_call | solution.py:575
  56.8 0.0 copy-done
  56.8 4.5 %shard_map.138 = f32[3072,512]{1,0:T(8,128)} custom-call(s32[12]{0:T(128)S(1)} %get-tuple-element.12.start_ref, f32[128,128]{1,0:T(8,128)S(1)} %get-tuple-element.13.rank_ref, bf16[2176,512]{1,0:T(8,128)(2,1)S(1)} %get-tuple-element.17.table_ref, f32[24,128]{1,0:T(8,128)S(1)} %get-tuple-element.18.inv_ref, f32[1,512]{1,0:T(1,128)S(1)} %bitcast.4), custom_call_target="tpu_custom_call" | custom-call | flops 1207959552 | bytes 6291456 | tf_op jit(solution)/shard_map/pallas_call | solution.py:676
Async XLA Ops:
  0.0 8.5 %copy-start.1 = (bf16[2048,512]{1,0:T(8,128)(2,1)S(1)}, bf16[2048,512]{1,0:T(8,128)(2,1)}, u32[]{:S(2)}) copy-start(bf16[2048,512]{1,0:T(8,128)(2,1)} %value_ref.1) | copy-start | bytes 6291460
  0.0 8.5 %copy-start.2 = (bf16[2048,512]{1,0:T(8,128)(2,1)S(1)}, bf16[2048,512]{1,0:T(8,128)(2,1)}, u32[]{:S(2)}) copy-start(bf16[2048,512]{1,0:T(8,128)(2,1)} %gate_ref.1) | copy-start | bytes 6291460
  0.0 8.5 %copy-start.3 = (bf16[2048,256]{1,0:T(8,128)(2,1)S(1)}, bf16[2048,256]{1,0:T(8,128)(2,1)}, u32[]{:S(2)}) copy-start(bf16[2048,256]{1,0:T(8,128)(2,1)} %state_ref.1) | copy-start | bytes 3145732
  0.0 8.5 %copy-start.4 = (bf16[2048,8]{0,1:T(8,128)(2,1)S(1)}, bf16[2048,8]{0,1:T(8,128)(2,1)}, u32[]{:S(2)}) copy-start(bf16[2048,8]{0,1:T(8,128)(2,1)} %param.19) | copy-start | bytes 98308
  0.0 8.5 %copy-start.5 = (f32[4,512]{1,0:T(4,128)S(1)}, f32[4,512]{1,0:T(4,128)}, u32[]{:S(2)}) copy-start(f32[4,512]{1,0:T(4,128)} %vconv_ref.1) | copy-start | bytes 24580
  0.0 8.5 %copy-start.6 = (f32[4,256]{1,0:T(4,128)S(1)}, f32[4,256]{1,0:T(4,128)}, u32[]{:S(2)}) copy-start(f32[4,256]{1,0:T(4,128)} %sconv_ref.1) | copy-start | bytes 12292
  0.0 8.5 %copy-start.7 = (f32[512]{0:T(512)S(1)}, f32[512]{0:T(512)}, u32[]{:S(2)}) copy-start(f32[512]{0:T(512)} %param.24) | copy-start | bytes 6148
  0.0 8.5 %copy-start.8 = (f32[256]{0:T(256)S(1)}, f32[256]{0:T(256)}, u32[]{:S(2)}) copy-start(f32[256]{0:T(256)} %param.26) | copy-start | bytes 3076
  0.1 8.5 %copy-start.9 = (f32[8]{0:T(128)S(1)}, f32[8]{0:T(128)}, u32[]{:S(2)}) copy-start(f32[8]{0:T(128)} %bias_ref.1) | copy-start | bytes 100
  0.1 8.5 %copy-start.10 = (f32[8]{0:T(128)S(1)}, f32[8]{0:T(128)}, u32[]{:S(2)}) copy-start(f32[8]{0:T(128)} %log_ref.1) | copy-start | bytes 100
  0.1 8.5 %copy-start.11 = (f32[8]{0:T(128)S(1)}, f32[8]{0:T(128)}, u32[]{:S(2)}) copy-start(f32[8]{0:T(128)} %skip_ref.1) | copy-start | bytes 100
  8.6 48.2 %copy-start = (f32[512]{0:T(512)S(1)}, f32[512]{0:T(512)}, u32[]{:S(2)}) copy-start(f32[512]{0:T(512)} %param.27) | copy-start | bytes 6148

commit v3 on v2

--- a/solution.py
+++ b/solution.py
@@ -19,6 +19,7 @@
 BLOCK = 256
 SPAN = BLOCK + 16
 UNROLL = 3
+JOINED = 1
 EPSILON = 1e-05
 LOG_FLOOR = -1e4
 MESH = pl.DeviceIdType.MESH
@@ -131,7 +132,12 @@
             rows_ref[pl.ds(pl.multiple_of(base + 16, 16), BLOCK), cols] = picked[16:]
         return carry
 
-    lax.fori_loop(0, blocks, step, 0)
+    def steps(i, carry):
+        for q in range(JOINED):
+            step(i * JOINED + q, 0)
+        return carry
+
+    lax.fori_loop(0, blocks // JOINED, steps, 0)
 
     clear = (start_ref[blocks - 1] // 16) * 16 + SPAN
 
@@ -206,6 +212,7 @@
     skip_ref,
     table,
     inv_ref,
+    ext_0,
     ext_a,
     ext_b,
     ext_h,
@@ -232,6 +239,7 @@
     ret_out,
     ret_in,
     entry,
+    base,
     squares,
     near_send,
     near_recv,
@@ -283,8 +291,8 @@
         return pltpu.make_async_remote_copy(
             src_ref=ends_out.at[lax.rem(to, 4)],
             dst_ref=ends_in.at[me],
-            send_sem=end_send.at[d],
-            recv_sem=end_recv.at[d],
+            send_sem=end_send,
+            recv_sem=end_recv,
             device_id={"ctx": to},
             device_id_type=MESH,
         )
@@ -294,8 +302,8 @@
         return pltpu.make_async_remote_copy(
             src_ref=out_slices.at[to],
             dst_ref=in_slices.at[me],
-            send_sem=out_send.at[d],
-            recv_sem=out_recv.at[d],
+            send_sem=out_send,
+            recv_sem=out_recv,
             device_id={"ctx": to},
             device_id_type=MESH,
         )
@@ -305,8 +313,8 @@
         return pltpu.make_async_remote_copy(
             src_ref=ret_out.at[to],
             dst_ref=ret_in.at[me],
-            send_sem=ret_send.at[d],
-            recv_sem=ret_recv.at[d],
+            send_sem=ret_send,
+            recv_sem=ret_recv,
             device_id={"ctx": to},
             device_id_type=MESH,
         )
@@ -315,8 +323,8 @@
         return pltpu.make_async_remote_copy(
             src_ref=squares.at[column],
             dst_ref=squares.at[column],
-            send_sem=sq_send.at[d],
-            recv_sem=sq_recv.at[d],
+            send_sem=sq_send,
+            recv_sem=sq_recv,
             device_id={"head": lax.rem(column + d, n_head)},
             device_id_type=MESH,
         )
@@ -324,8 +332,10 @@
     def start_all(copy, count):
         lax.fori_loop(1, count, lambda d, c: (copy(d).start(), c)[1], 0)
 
-    def wait_all(copy, count):
-        lax.fori_loop(1, count, lambda d, c: (copy(d).wait(), c)[1], 0)
+    def wait_all(sent, send_sem, landed, recv_sem):
+        for ref, sem in ((sent, send_sem), (landed, recv_sem)):
+            both = ref.at[pl.ds(0, landed.shape[0] - 1)]
+            pltpu.make_async_copy(both, both, sem).wait()
 
     for i in range(groups // 512):
         got = dot_nt(step_ref[...], rows_ref[i * 512 : (i + 1) * 512, :])
@@ -389,14 +399,12 @@
         taps[c, 0:4, :] = 0.5 * tap[:, at]
         taps[c, 4:5, :] = 0.5 * move[:, at]
 
-    def weights_of(n):
-        return value_ref[:, n * 256 : (n + 1) * 256] if n < 2 else state_ref[...]
-
-    def project(block, ext, n):
+    def project(block, ext):
         here = pl.ds(pl.multiple_of(block * big, big), big)
-        got = dot(rows_ref[here, :], weights_of(n))
-        ext[2 * n, 8 : 8 + big, :] = got[:, :128]
-        ext[2 * n + 1, 8 : 8 + big, :] = got[:, 128:]
+        for weights, first, count in ((value_ref, 0, 4), (state_ref, 4, 2)):
+            got = dot(rows_ref[here, :], weights[...])
+            for c in range(count):
+                ext[first + c, 8 : 8 + big, :] = got[:, c * 128 : (c + 1) * 128]
 
     def convolve(ext, c, at, length):
         h = taps[c, 4:5, :] + taps[c, 0:1, :] * ext[c, at + 5 : at + 5 + length, :]
@@ -404,8 +412,46 @@
             h = h + taps[c, j : j + 1, :] * ext[c, at + 5 + j : at + 5 + j + length, :]
         return h + h * jnp.tanh(h)
 
-    for n in range(3):
-        project(0, ext_a, n)
+    for k in (0, 2):
+        locs[k] = jnp.zeros((STATE, WIDE), F32)
+        fades[k] = jnp.ones((1, WIDE), F32)
+
+    def advance(block, ext, onto, target):
+        both = [dot_tn(lead_e[block * 2 + q], sel_e[...]) for q in range(2)]
+        if target is not None:
+            project(target, onto)
+        for q in range(2):
+            k = block * 2 + q
+            at = pl.ds(pl.multiple_of(k * T, T), T)
+            grow[k] = both[q][:, :WIDE]
+            weighted = []
+            for c in range(4):
+                x = convolve(ext, c, q * T, T)
+                xs[at, c * 128 : (c + 1) * 128] = x.astype(BF16)
+                tail = both[q][:, WIDE + c * 128 : WIDE + (c + 1) * 128]
+                weighted.append((x * tail).astype(BF16))
+            for c in range(2):
+                maps[at, c * 128 : (c + 1) * 128] = convolve(ext, 4 + c, q * T, T).astype(BF16)
+            new = dot_tn(maps[at, :STATE], jnp.concatenate(weighted, 1))
+            factor = both[q][T - 1 : T, :WIDE]
+            locs[k + 1] = factor * locs[k] + new
+            fades[k + 1] = factor * fades[k]
+
+    def hand_on(source, ext):
+        for c in range(6):
+            ext[c, 0:8, :] = source[c, big : big + 8, :]
+
+    def local(j, carry):
+        advance(2 * j + 1, ext_a, ext_b, 2 * j + 2)
+        hand_on(ext_a, ext_b)
+        advance(2 * j + 2, ext_b, ext_a, 2 * j + 3)
+        hand_on(ext_b, ext_a)
+        return carry
+
+    project(0, ext_0)
+    project(1, ext_a)
+    hand_on(ext_0, ext_a)
+    lax.fori_loop(0, bigs // 2 - 1, local, 0)
 
     near_copy(1).wait()
     near_copy(2).wait()
@@ -417,58 +463,20 @@
     shift = flag((row >= 12) & (lane >= 12) & (lane.astype(F32) == row.astype(F32) + few))
     halo = dot(shift, second.astype(BF16)) + jnp.where(iota(first.shape, 0) >= 12, first, 0.0)
     halo = halo.astype(BF16)
-    for n in range(3):
-        got = dot(halo, weights_of(n))
-        ext_h[2 * n, 8:24, :] = got[:, :128]
-        ext_h[2 * n + 1, 8:24, :] = got[:, 128:]
+    for weights, first, count in ((value_ref, 0, 4), (state_ref, 4, 2)):
+        got = dot(halo, weights[...])
+        for c in range(count):
+            ext_h[first + c, 8:24, :] = got[:, c * 128 : (c + 1) * 128]
     halo_gate[...] = silu(dot(halo, gate_ref[...]))
     for c in range(6):
         ext_h[c, 0:8, :] = jnp.zeros((8, 128), F32)
-        ext_a[c, 0:8, :] = ext_h[c, 16:24, :]
+        ext_0[c, 0:8, :] = ext_h[c, 16:24, :]
+    advance(bigs - 1, ext_a, None, None)
+    advance(0, ext_0, None, None)
     x_h = jnp.concatenate([convolve(ext_h, c, 0, 16) for c in range(4)], 1)
     c_h = convolve(ext_h, 5, 0, 16).astype(BF16)
 
-    locs[0] = jnp.zeros((STATE, WIDE), F32)
-    fades[0] = jnp.ones((1, WIDE), F32)
-
-    def advance(block, ext, onto, target):
-        for q in range(2):
-            k = block * 2 + q
-            at = pl.ds(pl.multiple_of(k * T, T), T)
-            if target is not None:
-                project(target, onto, 2 * q)
-                if q == 0:
-                    project(target, onto, 1)
-            both = dot_tn(lead_e[k], sel_e[...])
-            grow[k] = both[:, :WIDE]
-            weighted = []
-            for c in range(4):
-                x = convolve(ext, c, q * T, T)
-                xs[at, c * 128 : (c + 1) * 128] = x.astype(BF16)
-                tail = both[:, WIDE + c * 128 : WIDE + (c + 1) * 128]
-                weighted.append((x * tail).astype(BF16))
-            for c in range(2):
-                maps[at, c * 128 : (c + 1) * 128] = convolve(ext, 4 + c, q * T, T).astype(BF16)
-            new = dot_tn(maps[at, :STATE], jnp.concatenate(weighted, 1))
-            factor = both[T - 1 : T, :WIDE]
-            locs[k + 1] = factor * locs[k] + new
-            fades[k + 1] = factor * fades[k]
-
-    def hand_on(source, ext):
-        for c in range(6):
-            ext[c, 0:8, :] = source[c, big : big + 8, :]
-
-    def local(j, carry):
-        advance(2 * j, ext_a, ext_b, 2 * j + 1)
-        hand_on(ext_a, ext_b)
-        advance(2 * j + 1, ext_b, ext_a, 2 * j + 2)
-        hand_on(ext_b, ext_a)
-        return carry
-
-    lax.fori_loop(0, bigs // 2 - 1, local, 0)
-    advance(bigs - 2, ext_a, ext_b, bigs - 1)
-    hand_on(ext_a, ext_b)
-    advance(bigs - 1, ext_b, None, None)
+    locs[subs] = locs[subs] + fades[subs] * locs[2]
 
     for k in range(n_ctx):
         r, c = (k // 4) * share, (k % 4) * 128
@@ -485,20 +493,22 @@
     def inside(i, carry):
         g0 = pl.multiple_of(i * big, big)
         here = pl.ds(g0, big)
-        open_gate[here, :] = silu(dot(rows_ref[here, :], gate_ref[...]))
+        parts = []
         for q in range(big // T):
             k = i * (big // T) + q
             at = pl.ds(pl.multiple_of(g0 + q * T, T), T)
-            x, m = xs[at, :], maps[at, :]
+            m = maps[at, :]
             scores = jnp.where(lower, dot_nt(m[:, STATE:], m[:, :STATE]), 0.0)
-            lows = minus[k]
-            tile = jnp.concatenate([lows] * HEADS_HERE, 1) * sel_d[...]
+            tile = jnp.concatenate([minus[k]] * HEADS_HERE, 1) * sel_d[...]
             right = jnp.concatenate([sel_d[...], tile], 0).astype(BF16)
-            spread = dot_tn(lead_t[k], right)
-            weight = jnp.exp(jnp.minimum(spread, 60.0))
-            weight = (weight * jnp.concatenate([scores] * HEADS_HERE, 1)).astype(BF16)
+            parts.append((at, scores, dot_tn(lead_t[k], right)))
+        opened = dot(rows_ref[here, :], gate_ref[...])
+        for at, scores, spread in parts:
+            x = xs[at, :]
             for p in range(HEADS_HERE // 2):
                 pair = x[:, p * T : (p + 1) * T]
+                weight = jnp.exp(jnp.minimum(spread[:, 2 * p * T : 2 * (p + 1) * T], 60.0))
+                weight = (weight * jnp.concatenate([scores, scores], 1)).astype(BF16)
                 stacked = jnp.concatenate(
                     [
                         jnp.where(left_half, pair, jnp.zeros_like(pair)),
@@ -506,16 +516,17 @@
                     ],
                     0,
                 )
-                got = dot(weight[:, 2 * p * T : 2 * (p + 1) * T], stacked)
+                got = dot(weight, stacked)
                 cols = slice(p * T, (p + 1) * T)
                 mix[at, cols] = got + skip[:, cols] * pair.astype(F32)
+        open_gate[here, :] = silu(opened)
         return carry
 
     half = bigs // 2
     lax.fori_loop(0, half, inside, 0)
 
-    wait_all(end_copy, n_ctx)
-    wait_all(out_copy, n_ctx)
+    wait_all(ends_in, end_send, ends_in, end_recv)
+    wait_all(out_slices, out_send, in_slices, out_recv)
     running = jnp.zeros((share, 128), F32)
     for i in range(n_ctx):
         ret_out[i] = running.astype(BF16)
@@ -527,7 +538,7 @@
 
     lax.fori_loop(half, bigs, inside, 0)
 
-    wait_all(ret_copy, n_ctx)
+    wait_all(ret_out, ret_send, ret_in, ret_recv)
     for k in range(n_ctx):
         r, c = (k // 4) * share, (k % 4) * 128
         entry[r : r + share, c : c + 128] = ret_in[k]
@@ -541,13 +552,14 @@
     mine = squares.at[column]
     mine[...] = jnp.zeros(mine.shape, F32)
     mine[0:1, :] = dot_nt(ones, power)[0:1, :]
-    entering = entry[...].astype(F32)
+    base[0] = entry[...].astype(F32)
+    base[1] = locs[2] + fades[2] * base[0]
 
     def outer(i, carry):
         for q in range(4):
             k = i * 4 + q
             at = pl.ds(pl.multiple_of(k * T, T), T)
-            state = (locs[k] + fades[k] * entering).astype(BF16)
+            state = (locs[k] + fades[k] * base[jnp.where(k > 2, 1, 0)]).astype(BF16)
             gated = mix[at, :] + grow[k] * dot(maps[at, STATE:], state)
             gated = gated * open_gate[at, :]
             table[pl.ds(pl.multiple_of((k + 1) * T, T), T), :] = gated.astype(BF16)
@@ -557,7 +569,7 @@
     lax.fori_loop(0, subs // 4, outer, 0)
     start_all(sq_copy, n_head)
 
-    wait_all(sq_copy, n_head)
+    wait_all(squares, sq_send, squares, sq_recv)
     power = squares[0]
     for i in range(1, n_head):
         power = power + squares[i]
@@ -578,6 +590,7 @@
         in_specs=[vmem] * 11 + [smem] * 3,
         out_specs=[vmem, vmem],
         scratch_shapes=[
+            pltpu.VMEM((6, 2 * T + 8, 128), F32),
             pltpu.VMEM((6, 2 * T + 8, 128), F32),
             pltpu.VMEM((6, 2 * T + 8, 128), F32),
             pltpu.VMEM((6, 24, 128), F32),
@@ -604,17 +617,18 @@
             pltpu.VMEM((n_ctx, share, 128), BF16),
             pltpu.VMEM((n_ctx, share, 128), BF16),
             pltpu.VMEM((STATE, WIDE), BF16),
+            pltpu.VMEM((2, STATE, WIDE), F32),
             pltpu.VMEM((n_head, lines, T), F32),
             sem((2,)),
             sem((2,)),
-            sem((n_ctx,)),
-            sem((n_ctx,)),
-            sem((n_ctx,)),
-            sem((n_ctx,)),
-            sem((n_ctx,)),
-            sem((n_ctx,)),
-            sem((n_head,)),
-            sem((n_head,)),
+            sem,
+            sem,
+            sem,
+            sem,
+            sem,
+            sem,
+            sem,
+            sem,
         ],
         compiler_params=pltpu.CompilerParams(
             collective_id=0, has_side_effects=True, vmem_limit_bytes=32 << 20

time: 61.8 us -> 55.2 us (0.89)
  Pallas kernels: 61.1 us -> 54.9 us
    pallas_call x1, Pallas kernels: 48.2 us -> 42.7 us  [layer(): pl.pallas_call(functools.partial(layer_kernel, n_ctx, n_head, groups), ou...]
    pallas_call x1, Pallas kernels: 8.36 us -> 7.64 us  [compact(): pl.pallas_call(functools.partial(compact_kernel, groups), out_shape=[on_c...]
where the time goes in v3:
time: 55.2 us; the launch traced here: 55.1 us
  Pallas kernels  54.9 us (99%)
    pallas_call x1, Pallas kernels, layer(): pl.pallas_call(functools.partial(layer_kernel, n_ctx, n_head, groups), ou...  42.7 us
    pallas_call x1, Pallas kernels, compact(): pl.pallas_call(functools.partial(compact_kernel, groups), out_shape=[on_c...  7.64 us
    pallas_call x1, Pallas kernels, expand(): pl.pallas_call(functools.partial(expand_kernel, groups), out_shape=jax.Sh...  4.53 us

profile of v3, /device:TPU:1, one launch (start us, length us, event | category | flops | bytes accessed | tf_op | source)
XLA Modules:
  0.0 55.1 jit_solution(3828018369318029108)
XLA Ops:
  0.0 0.0 copy-start.1
  0.0 0.0 copy-start.2
  0.0 0.0 copy-start.3
  0.0 0.0 copy-start.4
  0.0 0.0 copy-start.5
  0.0 0.0 copy-start.6
  0.0 0.0 copy-start.7
  0.0 0.0 copy-start.8
  0.1 0.0 copy-start.9
  0.1 0.0 copy-start.10
  0.1 0.0 copy-start.11
  0.1 7.6 %shard_map.136 = (bf16[2320,2048]{1,0:T(8,128)(2,1)S(1)}, bf16[16,2048]{1,0:T(8,128)(2,1)S(1)}, s32[8,128]{1,0:T(8,128)S(1)}, f32[128,128]{1,0:T(8,128)S(1)}, s32[12]{0:T(128)S(1)}) custom-call(s32[3072]{0:T(1024)} %bnd_hbm.1, bf16[3072,2048]{1,0:T(8,128)(2,1)} %bytes_hbm.1), custom_call_target="tpu_custom_call" | custom-call | flops 3422552064 | bytes 12582912 | tf_op jit(solution)/shard_map/pallas_call | solution.py:162
  7.7 0.0 copy-done.1
  7.7 0.0 copy-done.2
  7.8 0.0 copy-done.3
  7.8 0.0 copy-done.4
  7.8 0.0 copy-done.5
  7.8 0.0 copy-done.6
  7.8 0.0 copy-done.7
  7.8 0.0 copy-done.8
  7.8 0.0 copy-done.9
  7.8 0.0 copy-done.10
  7.8 0.0 copy-done.11
  7.8 0.0 copy-start
  7.9 42.7 %shard_map.137 = (bf16[2176,512]{1,0:T(8,128)(2,1)S(1)}, f32[24,128]{1,0:T(8,128)S(1)}) custom-call(bf16[2320,2048]{1,0:T(8,128)(2,1)S(1)} %get-tuple-element.14.rows_ref, bf16[16,2048]{1,0:T(8,128)(2,1)S(1)} %get-tuple-element.15.tail_ref, s32[8,128]{1,0:T(8,128)S(1)} %get-tuple-element.16.count_ref, bf16[2048,512]{1,0:T(8,128)(2,1)S(1)} %copy-done.1, ...), custom_call_target="tpu_custom_call" | custom-call | flops 12884901888 | bytes 8388608 | tf_op jit(solution)/shard_map/pallas_call | solution.py:587
  50.6 0.0 copy-done
  50.6 4.5 %shard_map.138 = f32[3072,512]{1,0:T(8,128)} custom-call(s32[12]{0:T(128)S(1)} %get-tuple-element.12.start_ref, f32[128,128]{1,0:T(8,128)S(1)} %get-tuple-element.13.rank_ref, bf16[2176,512]{1,0:T(8,128)(2,1)S(1)} %get-tuple-element.17.table_ref, f32[24,128]{1,0:T(8,128)S(1)} %get-tuple-element.18.inv_ref, f32[1,512]{1,0:T(1,128)S(1)} %bitcast.4), custom_call_target="tpu_custom_call" | custom-call | flops 1207959552 | bytes 6291456 | tf_op jit(solution)/shard_map/pallas_call | solution.py:690
Async XLA Ops:
  0.0 7.7 %copy-start.1 = (bf16[2048,512]{1,0:T(8,128)(2,1)S(1)}, bf16[2048,512]{1,0:T(8,128)(2,1)}, u32[]{:S(2)}) copy-start(bf16[2048,512]{1,0:T(8,128)(2,1)} %value_ref.1) | copy-start | bytes 6291460
  0.0 7.7 %copy-start.2 = (bf16[2048,512]{1,0:T(8,128)(2,1)S(1)}, bf16[2048,512]{1,0:T(8,128)(2,1)}, u32[]{:S(2)}) copy-start(bf16[2048,512]{1,0:T(8,128)(2,1)} %gate_ref.1) | copy-start | bytes 6291460
  0.0 7.8 %copy-start.3 = (bf16[2048,256]{1,0:T(8,128)(2,1)S(1)}, bf16[2048,256]{1,0:T(8,128)(2,1)}, u32[]{:S(2)}) copy-start(bf16[2048,256]{1,0:T(8,128)(2,1)} %state_ref.1) | copy-start | bytes 3145732
  0.0 7.8 %copy-start.4 = (bf16[2048,8]{0,1:T(8,128)(2,1)S(1)}, bf16[2048,8]{0,1:T(8,128)(2,1)}, u32[]{:S(2)}) copy-start(bf16[2048,8]{0,1:T(8,128)(2,1)} %param.19) | copy-start | bytes 98308
  0.0 7.8 %copy-start.5 = (f32[4,512]{1,0:T(4,128)S(1)}, f32[4,512]{1,0:T(4,128)}, u32[]{:S(2)}) copy-start(f32[4,512]{1,0:T(4,128)} %vconv_ref.1) | copy-start | bytes 24580
  0.0 7.8 %copy-start.6 = (f32[4,256]{1,0:T(4,128)S(1)}, f32[4,256]{1,0:T(4,128)}, u32[]{:S(2)}) copy-start(f32[4,256]{1,0:T(4,128)} %sconv_ref.1) | copy-start | bytes 12292
  0.0 7.8 %copy-start.7 = (f32[512]{0:T(512)S(1)}, f32[512]{0:T(512)}, u32[]{:S(2)}) copy-start(f32[512]{0:T(512)} %param.24) | copy-start | bytes 6148
  0.0 7.8 %copy-start.8 = (f32[256]{0:T(256)S(1)}, f32[256]{0:T(256)}, u32[]{:S(2)}) copy-start(f32[256]{0:T(256)} %param.26) | copy-start | bytes 3076
  0.1 7.8 %copy-start.9 = (f32[8]{0:T(128)S(1)}, f32[8]{0:T(128)}, u32[]{:S(2)}) copy-start(f32[8]{0:T(128)} %bias_ref.1) | copy-start | bytes 100
  0.1 7.8 %copy-start.10 = (f32[8]{0:T(128)S(1)}, f32[8]{0:T(128)}, u32[]{:S(2)}) copy-start(f32[8]{0:T(128)} %log_ref.1) | copy-start | bytes 100
  0.1 7.8 %copy-start.11 = (f32[8]{0:T(128)S(1)}, f32[8]{0:T(128)}, u32[]{:S(2)}) copy-start(f32[8]{0:T(128)} %skip_ref.1) | copy-start | bytes 100
  7.8 42.7 %copy-start = (f32[512]{0:T(512)S(1)}, f32[512]{0:T(512)}, u32[]{:S(2)}) copy-start(f32[512]{0:T(512)} %param.27) | copy-start | bytes 6148

commit v4 on v3

--- a/solution.py
+++ b/solution.py
@@ -177,7 +177,7 @@
             pltpu.SemaphoreType.DMA((blocks,)),
             pltpu.SemaphoreType.DMA,
         ],
-        compiler_params=pltpu.CompilerParams(vmem_limit_bytes=30 << 20),
+        compiler_params=pltpu.CompilerParams(vmem_limit_bytes=18 << 20),
         cost_estimate=pl.CostEstimate(
             flops=2 * SPAN * length * width, bytes_accessed=2 * length * width, transcendentals=0
         ),
@@ -192,9 +192,18 @@
     return out
 
 
+def start_all(copy, count):
+    lax.fori_loop(1, count, lambda d, c: (copy(d).start(), c)[1], 0)
+
+
+def wait_all(sent, send_sem, landed, recv_sem):
+    for ref, sem in ((sent, send_sem), (landed, recv_sem)):
+        both = ref.at[pl.ds(0, landed.shape[0] - 1)]
+        pltpu.make_async_copy(both, both, sem).wait()
+
+
 def layer_kernel(
     n_ctx,
-    n_head,
     groups,
     rows_ref,
     tail_ref,
@@ -210,20 +219,20 @@
     bias_ref,
     log_ref,
     skip_ref,
-    table,
-    inv_ref,
+    mix,
+    open_gate,
+    grow,
+    locs,
+    fades,
+    maps,
+    base,
+    lead_ref,
     ext_0,
     ext_a,
     ext_b,
     ext_h,
     taps,
     xs,
-    maps,
-    mix,
-    open_gate,
-    grow,
-    locs,
-    fades,
     raw_step,
     lead_t,
     lead_e,
@@ -239,8 +248,6 @@
     ret_out,
     ret_in,
     entry,
-    base,
-    squares,
     near_send,
     near_recv,
     end_send,
@@ -249,11 +256,8 @@
     out_recv,
     ret_send,
     ret_recv,
-    sq_send,
-    sq_recv,
 ):
     me = lax.axis_index("ctx")
-    column = lax.axis_index("head")
     subs = groups // T
     share = STATE * 4 // n_ctx
     big = 2 * T
@@ -267,14 +271,7 @@
         )
         return carry
 
-    def greet_head(d, carry):
-        pl.semaphore_signal(
-            barrier, inc=1, device_id={"head": lax.rem(column + d, n_head)}, device_id_type=MESH
-        )
-        return carry
-
     lax.fori_loop(1, n_ctx, greet_ctx, 0)
-    lax.fori_loop(1, n_head, greet_head, 0)
 
     def near_copy(d):
         return pltpu.make_async_remote_copy(
@@ -319,31 +316,13 @@
             device_id_type=MESH,
         )
 
-    def sq_copy(d):
-        return pltpu.make_async_remote_copy(
-            src_ref=squares.at[column],
-            dst_ref=squares.at[column],
-            send_sem=sq_send,
-            recv_sem=sq_recv,
-            device_id={"head": lax.rem(column + d, n_head)},
-            device_id_type=MESH,
-        )
-
-    def start_all(copy, count):
-        lax.fori_loop(1, count, lambda d, c: (copy(d).start(), c)[1], 0)
-
-    def wait_all(sent, send_sem, landed, recv_sem):
-        for ref, sem in ((sent, send_sem), (landed, recv_sem)):
-            both = ref.at[pl.ds(0, landed.shape[0] - 1)]
-            pltpu.make_async_copy(both, both, sem).wait()
-
     for i in range(groups // 512):
         got = dot_nt(step_ref[...], rows_ref[i * 512 : (i + 1) * 512, :])
         for q in range(4):
             k = i * 4 + q
             raw_step[k * 8 : (k + 1) * 8, :] = got[:, q * T : (q + 1) * T]
 
-    pl.semaphore_wait(barrier, n_ctx - 1 + n_head - 1)
+    pl.semaphore_wait(barrier, n_ctx - 1)
     near_copy(1).start()
     near_copy(2).start()
 
@@ -543,17 +522,71 @@
         r, c = (k // 4) * share, (k % 4) * 128
         entry[r : r + share, c : c + 128] = ret_in[k]
 
+    base[0] = entry[...].astype(F32)
+    base[1] = locs[2] + fades[2] * base[0]
+    y_h = dot(c_h, entry[...]) + skip * x_h
+    lead_ref[...] = y_h * halo_gate[...]
+
+
+def line_of(start, groups):
+    return jnp.minimum((start + T - 1) // T, (groups + T - window_of(groups)) // T)
+
+
+def window_of(groups):
+    return min(3 * T, groups + T)
+
+
+def norm_kernel(
+    n_head,
+    groups,
+    mix,
+    open_gate,
+    grow,
+    locs,
+    fades,
+    maps,
+    base,
+    lead_ref,
+    rank_ref,
+    start_ref,
+    table,
+    inv_ref,
+    place_ref,
+    squares,
+    sq_send,
+    sq_recv,
+):
+    column = lax.axis_index("head")
+    subs = groups // T
+    blocks = place_ref.shape[0] // BLOCK
+    barrier = pltpu.get_barrier_semaphore()
+
+    def greet_head(d, carry):
+        pl.semaphore_signal(
+            barrier, inc=1, device_id={"head": lax.rem(column + d, n_head)}, device_id_type=MESH
+        )
+        return carry
+
+    lax.fori_loop(1, n_head, greet_head, 0)
+
+    def sq_copy(d):
+        return pltpu.make_async_remote_copy(
+            src_ref=squares.at[column],
+            dst_ref=squares.at[column],
+            send_sem=sq_send,
+            recv_sem=sq_recv,
+            device_id={"head": lax.rem(column + d, n_head)},
+            device_id_type=MESH,
+        )
+
     ones = jnp.ones((8, WIDE), BF16)
-    y_h = dot(c_h, entry[...]) + skip * x_h
-    g_h = y_h * halo_gate[...]
+    g_h = lead_ref[...]
     table[0 : T - 16, :] = jnp.zeros((T - 16, WIDE), BF16)
     table[T - 16 : T, :] = g_h.astype(BF16)
     power = jnp.concatenate([jnp.zeros((T - 16, WIDE), F32), g_h * g_h], 0).astype(BF16)
     mine = squares.at[column]
     mine[...] = jnp.zeros(mine.shape, F32)
     mine[0:1, :] = dot_nt(ones, power)[0:1, :]
-    base[0] = entry[...].astype(F32)
-    base[1] = locs[2] + fades[2] * base[0]
 
     def outer(i, carry):
         for q in range(4):
@@ -567,7 +600,26 @@
         return carry
 
     lax.fori_loop(0, subs // 4, outer, 0)
+
+    pl.semaphore_wait(barrier, n_head - 1)
     start_all(sq_copy, n_head)
+
+    def locate(i, carry):
+        for j in (2 * i, 2 * i + 1) if blocks % 2 == 0 else (i,):
+            for half in range(2):
+                lane = iota((T, T), 1)
+                rank = jnp.sum(
+                    jnp.where(lane == 2 * j + half, rank_ref[...], 0.0), axis=1, keepdims=True
+                )
+                first = (line_of(start_ref[j], groups) * T).astype(F32)
+                place = jnp.broadcast_to(rank + ((T - 1.0) - first), (T, T))
+                lane = lane.astype(F32)
+                hits = [flag(place == lane + w * T) for w in range(window_of(groups) // T)]
+                at = pl.ds(pl.multiple_of(j * BLOCK + half * T, T), T)
+                place_ref[at, :] = jnp.concatenate(hits, 1)
+        return carry
+
+    lax.fori_loop(0, blocks // 2 if blocks % 2 == 0 else blocks, locate, 0)
 
     wait_all(squares, sq_send, squares, sq_recv)
     power = squares[0]
@@ -576,19 +628,54 @@
     inv_ref[...] = lax.rsqrt(power * (1.0 / (n_head * WIDE)) + EPSILON)
 
 
-def layer(n_ctx, n_head, groups, *args):
+def norm(n_head, groups, length, *args):
+    subs = groups // T
+    lines = -(-(subs + 1) // 8) * 8
+    vmem = pl.BlockSpec(memory_space=pltpu.VMEM)
+    return pl.pallas_call(
+        functools.partial(norm_kernel, n_head, groups),
+        out_shape=[
+            on_chip((groups + T, WIDE), BF16),
+            on_chip((lines, T), F32),
+            on_chip((length, window_of(groups)), BF16),
+        ],
+        in_specs=[vmem] * 9 + [pl.BlockSpec(memory_space=pltpu.SMEM)],
+        out_specs=[vmem] * 3,
+        scratch_shapes=[
+            pltpu.VMEM((n_head, lines, T), F32),
+            pltpu.SemaphoreType.DMA,
+            pltpu.SemaphoreType.DMA,
+        ],
+        compiler_params=pltpu.CompilerParams(
+            collective_id=1, has_side_effects=True, vmem_limit_bytes=8 << 20
+        ),
+        cost_estimate=pl.CostEstimate(
+            flops=4 * groups * STATE * WIDE, bytes_accessed=1 << 20, transcendentals=0
+        ),
+    )(*args)
+
+
+def layer(n_ctx, groups, *args):
     subs = groups // T
     share = STATE * 4 // n_ctx
-    lines = -(-(subs + 1) // 8) * 8
     vmem = pl.BlockSpec(memory_space=pltpu.VMEM)
     smem = pl.BlockSpec(memory_space=pltpu.SMEM)
     width = args[0].shape[1]
     sem = pltpu.SemaphoreType.DMA
     return pl.pallas_call(
-        functools.partial(layer_kernel, n_ctx, n_head, groups),
-        out_shape=[on_chip((groups + T, WIDE), BF16), on_chip((lines, T), F32)],
+        functools.partial(layer_kernel, n_ctx, groups),
+        out_shape=[
+            on_chip((groups, WIDE), F32),
+            on_chip((groups, WIDE), F32),
+            on_chip((subs, T, WIDE), F32),
+            on_chip((subs + 1, STATE, WIDE), F32),
+            on_chip((subs + 1, 1, WIDE), F32),
+            on_chip((groups, 2 * STATE), BF16),
+            on_chip((2, STATE, WIDE), F32),
+            on_chip((16, WIDE), F32),
+        ],
         in_specs=[vmem] * 11 + [smem] * 3,
-        out_specs=[vmem, vmem],
+        out_specs=[vmem] * 8,
         scratch_shapes=[
             pltpu.VMEM((6, 2 * T + 8, 128), F32),
             pltpu.VMEM((6, 2 * T + 8, 128), F32),
@@ -596,12 +683,6 @@
             pltpu.VMEM((6, 24, 128), F32),
             pltpu.VMEM((6, 8, 128), F32),
             pltpu.VMEM((groups, WIDE), BF16),
-            pltpu.VMEM((groups, 2 * STATE), BF16),
-            pltpu.VMEM((groups, WIDE), F32),
-            pltpu.VMEM((groups, WIDE), F32),
-            pltpu.VMEM((subs, T, WIDE), F32),
-            pltpu.VMEM((subs + 1, STATE, WIDE), F32),
-            pltpu.VMEM((subs + 1, 1, WIDE), F32),
             pltpu.VMEM((subs * 8, T), F32),
             pltpu.VMEM((subs, 48, T), BF16),
             pltpu.VMEM((subs, 32, T), BF16),
@@ -617,8 +698,6 @@
             pltpu.VMEM((n_ctx, share, 128), BF16),
             pltpu.VMEM((n_ctx, share, 128), BF16),
             pltpu.VMEM((STATE, WIDE), BF16),
-            pltpu.VMEM((2, STATE, WIDE), F32),
-            pltpu.VMEM((n_head, lines, T), F32),
             sem((2,)),
             sem((2,)),
             sem,
@@ -627,11 +706,9 @@
             sem,
             sem,
             sem,
-            sem,
-            sem,
         ],
         compiler_params=pltpu.CompilerParams(
-            collective_id=0, has_side_effects=True, vmem_limit_bytes=32 << 20
+            collective_id=0, has_side_effects=True, vmem_limit_bytes=14 << 20
         ),
         cost_estimate=pl.CostEstimate(
             flops=2 * groups * width * 1536, bytes_accessed=8 << 20, transcendentals=1 << 22
@@ -639,35 +716,23 @@
     )(*args)
 
 
-def expand_kernel(
-    groups, start_ref, rank_ref, table_ref, inv_ref, gain_ref, out_hbm, ready, sems
-):
+def expand_kernel(groups, start_ref, place_ref, table_ref, inv_ref, gain_ref, out_hbm, ready, sems):
     blocks = out_hbm.shape[0] // BLOCK
-    window = min(3 * T, groups + T)
+    window = window_of(groups)
 
     def send(j):
         at = pl.ds(pl.multiple_of(j * BLOCK, BLOCK), BLOCK)
         return pltpu.make_async_copy(ready.at[at], out_hbm.at[at], sems.at[j])
 
     def step(j, carry):
-        line = jnp.minimum((start_ref[j] + T - 1) // T, (groups + T - window) // T)
-        base = pl.multiple_of(line * T, T)
-        lane = iota((T, T), 1)
-        places, scales = [], []
-        for half in range(2):
-            rank = jnp.sum(
-                jnp.where(lane == 2 * j + half, rank_ref[...], 0.0), axis=1, keepdims=True
-            )
-            place = jnp.broadcast_to(rank.astype(I32) + (T - 1) - base, (T, T))
-            hits = [place == lane + w * T for w in range(window // T)]
-            places.append(jnp.concatenate([flag(hit) for hit in hits], 1))
-            scale = jnp.zeros((T, T), F32)
-            for w, hit in enumerate(hits):
-                scale = jnp.where(hit, inv_ref[pl.ds(line + w, 1), :], scale)
-            scales.append(jnp.sum(scale, axis=1, keepdims=True))
-        got = dot(jnp.concatenate(places, 0), table_ref[pl.ds(base, window), :])
-        got = got * gain_ref[...] * jnp.concatenate(scales, 0)
-        ready[pl.ds(pl.multiple_of(j * BLOCK, BLOCK), BLOCK), :] = got
+        line = line_of(start_ref[j], groups)
+        at = pl.ds(pl.multiple_of(j * BLOCK, BLOCK), BLOCK)
+        places = place_ref[at, :]
+        got = dot(places, table_ref[pl.ds(pl.multiple_of(line * T, T), window), :])
+        scale = jnp.zeros((BLOCK, T), F32)
+        for w in range(window // T):
+            scale = scale + places[:, w * T : (w + 1) * T].astype(F32) * inv_ref[pl.ds(line + w, 1), :]
+        ready[at, :] = got * gain_ref[...] * jnp.sum(scale, axis=1, keepdims=True)
         send(j).start()
         return carry
 
@@ -685,7 +750,7 @@
     lax.fori_loop(0, blocks, finish, 0)
 
 
-def expand(length, groups, starts, rank, table, inv, gain):
+def expand(length, groups, starts, places, table, inv, gain):
     vmem = pl.BlockSpec(memory_space=pltpu.VMEM)
     return pl.pallas_call(
         functools.partial(expand_kernel, groups),
@@ -696,11 +761,11 @@
             pltpu.VMEM((length, WIDE), F32),
             pltpu.SemaphoreType.DMA((length // BLOCK,)),
         ],
-        compiler_params=pltpu.CompilerParams(vmem_limit_bytes=24 << 20),
+        compiler_params=pltpu.CompilerParams(vmem_limit_bytes=12 << 20),
         cost_estimate=pl.CostEstimate(
             flops=2 * length * 3 * T * WIDE, bytes_accessed=4 * length * WIDE, transcendentals=0
         ),
-    )(starts, rank, table, inv, gain)
+    )(starts, places, table, inv, gain)
 
 
 def shards(
@@ -725,9 +790,8 @@
     rows, tail, count, rank, starts = compact(
         keep_off_chip(boundary), keep_off_chip(byte_rows), groups
     )
-    table, inv = layer(
+    carried = layer(
         n_ctx,
-        n_head,
         groups,
         rows,
         tail,
@@ -741,7 +805,9 @@
         decay_log,
         skip_gain,
     )
-    return expand(byte_rows.shape[0], groups, starts, rank, table, inv, norm_gain.reshape(1, -1))
+    length = byte_rows.shape[0]
+    table, inv, places = norm(n_head, groups, length, *carried, rank, starts)
+    return expand(length, groups, starts, places, table, inv, norm_gain.reshape(1, -1))
 
 
 def solution(mesh, groups=2048):

time: 55.2 us -> 55.8 us (1.011)
  Pallas kernels: 54.9 us -> 55.5 us
    pallas_call x1 -> x2, Pallas kernels: 42.7 us -> 43.5 us  [the longest x1 31.5 us: layer(): pl.pallas_call(functools.partial(layer_kernel, n_ctx, groups), out_shape=...]
    pallas_call x1, Pallas kernels: 4.53 us -> 3.94 us  [expand(): pl.pallas_call(functools.partial(expand_kernel, groups), out_shape=jax.Sh...]
where the time goes in v4:
time: 55.8 us; the launch traced here: 55.7 us
  Pallas kernels  55.5 us (99%)
    pallas_call x1, Pallas kernels, layer(): pl.pallas_call(functools.partial(layer_kernel, n_ctx, groups), out_shape=...  31.5 us
    pallas_call x1, Pallas kernels, norm(): pl.pallas_call(functools.partial(norm_kernel, n_head, groups), out_shape=...  12 us
    pallas_call x1, Pallas kernels, compact(): pl.pallas_call(functools.partial(compact_kernel, groups), out_shape=[on_c...  7.98 us
    pallas_call x1, Pallas kernels, expand(): pl.pallas_call(functools.partial(expand_kernel, groups), out_shape=jax.Sh...  3.94 us

profile of v4, /device:TPU:1, one launch (start us, length us, event | category | flops | bytes accessed | tf_op | source)
XLA Modules:
  0.0 55.7 jit_solution(4688884401075330812)
XLA Ops:
  0.0 0.0 copy-start.1
  0.0 0.0 copy-start.2
  0.0 0.0 copy-start.3
  0.0 0.0 copy-start.4
  0.0 0.0 copy-start.5
  0.0 0.0 copy-start.6
  0.0 0.0 copy-start.7
  0.0 0.0 copy-start.8
  0.1 0.0 copy-start.9
  0.1 0.0 copy-start.10
  0.1 0.0 copy-start.11
  0.1 8.0 %shard_map.136 = (bf16[2320,2048]{1,0:T(8,128)(2,1)S(1)}, bf16[16,2048]{1,0:T(8,128)(2,1)S(1)}, s32[8,128]{1,0:T(8,128)S(1)}, f32[128,128]{1,0:T(8,128)S(1)}, s32[12]{0:T(128)S(1)}) custom-call(s32[3072]{0:T(1024)} %bnd_hbm.1, bf16[3072,2048]{1,0:T(8,128)(2,1)} %bytes_hbm.1), custom_call_target="tpu_custom_call" | custom-call | flops 3422552064 | bytes 12582912 | tf_op jit(solution)/shard_map/pallas_call | solution.py:162
  8.1 0.0 copy-done.1
  8.1 0.0 copy-done.2
  8.1 0.0 copy-done.3
  8.1 0.0 copy-done.4
  8.1 0.0 copy-done.5
  8.1 0.0 copy-done.6
  8.1 0.0 copy-done.7
  8.1 0.0 copy-done.8
  8.2 0.0 copy-done.9
  8.2 0.0 copy-done.10
  8.2 0.0 copy-done.11
  8.2 31.5 %shard_map.137 = (f32[2048,512]{1,0:T(8,128)S(1)}, f32[2048,512]{1,0:T(8,128)S(1)}, f32[16,128,512]{2,1,0:T(8,128)S(1)}, f32[17,128,512]{2,1,0:T(8,128)S(1)}, f3...) custom-call(bf16[2320,2048]{1,0:T(8,128)(2,1)S(1)} %get-tuple-elemen, ...), custom_call_target="tpu_custom_call" | custom-call | flops 12884901888 | bytes 8388608 | tf_op jit(solution)/shard_map/pallas_call | solution.py:665
  39.7 0.0 copy-start
  39.8 12.0 %shard_map.138 = (bf16[2176,512]{1,0:T(8,128)(2,1)S(1)}, f32[24,128]{1,0:T(8,128)S(1)}, bf16[3072,384]{1,0:T(8,128)(2,1)S(1)}) custom-call(f32[2048,512]{1,0:T(8,128)S(1)} %get-tuple-element.25.mix, f32[2048,512]{1,0:T(8,128)S(1)} %get-tuple-element.26.open_gate, f32[16,128,512]{2,1,0:T(8,128)S(1)} %get-tuple-element.27.grow, ...), custom_call_target="tpu_custom_call" | custom-call | flops 536870912 | bytes 1048576 | tf_op jit(solution)/shard_map/pallas_call | solution.py:635
  51.8 0.0 copy-done
  51.8 3.9 %shard_map.139 = f32[3072,512]{1,0:T(8,128)} custom-call(s32[12]{0:T(128)S(1)} %get-tuple-element.21.start_ref, bf16[3072,384]{1,0:T(8,128)(2,1)S(1)} %get-tuple-element.34.place_ref, bf16[2176,512]{1,0:T(8,128)(2,1)S(1)} %get-tuple-element.35.table_ref, f32[24,128]{1,0:T(8,128)S(1)} %get-tuple-element.36.inv_ref, f32[1,512]{1,0:T(1,128)S(1)} %bitcast.4), custom_call_target="tpu_custom_call" | custom-call | flops 1207959552 | bytes 6291456 | tf_op jit(solution)/shard_map/pallas_call | solution.py:755
Async XLA Ops:
  0.0 8.1 %copy-start.1 = (bf16[2048,512]{1,0:T(8,128)(2,1)S(1)}, bf16[2048,512]{1,0:T(8,128)(2,1)}, u32[]{:S(2)}) copy-start(bf16[2048,512]{1,0:T(8,128)(2,1)} %value_ref.1) | copy-start | bytes 6291460
  0.0 8.1 %copy-start.2 = (bf16[2048,512]{1,0:T(8,128)(2,1)S(1)}, bf16[2048,512]{1,0:T(8,128)(2,1)}, u32[]{:S(2)}) copy-start(bf16[2048,512]{1,0:T(8,128)(2,1)} %gate_ref.1) | copy-start | bytes 6291460
  0.0 8.1 %copy-start.3 = (bf16[2048,256]{1,0:T(8,128)(2,1)S(1)}, bf16[2048,256]{1,0:T(8,128)(2,1)}, u32[]{:S(2)}) copy-start(bf16[2048,256]{1,0:T(8,128)(2,1)} %state_ref.1) | copy-start | bytes 3145732
  0.0 8.1 %copy-start.4 = (bf16[2048,8]{0,1:T(8,128)(2,1)S(1)}, bf16[2048,8]{0,1:T(8,128)(2,1)}, u32[]{:S(2)}) copy-start(bf16[2048,8]{0,1:T(8,128)(2,1)} %param.19) | copy-start | bytes 98308
  0.0 8.1 %copy-start.5 = (f32[4,512]{1,0:T(4,128)S(1)}, f32[4,512]{1,0:T(4,128)}, u32[]{:S(2)}) copy-start(f32[4,512]{1,0:T(4,128)} %vconv_ref.1) | copy-start | bytes 24580
  0.0 8.1 %copy-start.6 = (f32[4,256]{1,0:T(4,128)S(1)}, f32[4,256]{1,0:T(4,128)}, u32[]{:S(2)}) copy-start(f32[4,256]{1,0:T(4,128)} %sconv_ref.1) | copy-start | bytes 12292
  0.0 8.1 %copy-start.7 = (f32[512]{0:T(512)S(1)}, f32[512]{0:T(512)}, u32[]{:S(2)}) copy-start(f32[512]{0:T(512)} %param.24) | copy-start | bytes 6148
  0.0 8.1 %copy-start.8 = (f32[256]{0:T(256)S(1)}, f32[256]{0:T(256)}, u32[]{:S(2)}) copy-start(f32[256]{0:T(256)} %param.26) | copy-start | bytes 3076
  0.1 8.1 %copy-start.9 = (f32[8]{0:T(128)S(1)}, f32[8]{0:T(128)}, u32[]{:S(2)}) copy-start(f32[8]{0:T(128)} %bias_ref.1) | copy-start | bytes 100
  0.1 8.1 %copy-start.10 = (f32[8]{0:T(128)S(1)}, f32[8]{0:T(128)}, u32[]{:S(2)}) copy-start(f32[8]{0:T(128)} %log_ref.1) | copy-start | bytes 100
  0.1 8.1 %copy-start.11 = (f32[8]{0:T(128)S(1)}, f32[8]{0:T(128)}, u32[]{:S(2)}) copy-start(f32[8]{0:T(128)} %skip_ref.1) | copy-start | bytes 100
  39.7 12.0 %copy-start = (f32[512]{0:T(512)S(1)}, f32[512]{0:T(512)}, u32[]{:S(2)}) copy-start(f32[512]{0:T(512)} %param.27) | copy-start | bytes 6148

commit v5 on v4

--- a/solution.py
+++ b/solution.py
@@ -322,10 +322,6 @@
             k = i * 4 + q
             raw_step[k * 8 : (k + 1) * 8, :] = got[:, q * T : (q + 1) * T]
 
-    pl.semaphore_wait(barrier, n_ctx - 1)
-    near_copy(1).start()
-    near_copy(2).start()
-
     shape = (subs * 8, T)
     raw = raw_step[...] + head_column(bias_ref, shape)
     soft = jnp.maximum(raw, 0.0) + jnp.log1p(jnp.exp(-jnp.abs(raw)))
@@ -336,6 +332,20 @@
     tri = flag(iota((T, T), 0) <= iota((T, T), 1))
     d0, d1, d2 = pieces(decay, 3)
     cum = (dot(d0.astype(BF16), tri) + dot(d1.astype(BF16), tri)) + dot(d2.astype(BF16), tri)
+    def project(block, ext):
+        here = pl.ds(pl.multiple_of(block * big, big), big)
+        for weights, first, count in ((value_ref, 0, 4), (state_ref, 4, 2)):
+            got = dot(rows_ref[here, :], weights[...])
+            for c in range(count):
+                ext[first + c, 8 : 8 + big, :] = got[:, c * 128 : (c + 1) * 128]
+
+    def hand_on(source, ext):
+        for c in range(6):
+            ext[c, 0:8, :] = source[c, big : big + 8, :]
+
+    project(0, ext_0)
+    project(1, ext_a)
+    hand_on(ext_0, ext_a)
     total = jnp.broadcast_to(cum[:, T - 1 : T], shape)
     cums = pieces(cum, 3)
     lows = pieces(logs - cum, 3)
@@ -357,8 +367,6 @@
             for part in (high, low)
         ]
         ends_out[c] = jnp.concatenate(both, 0).astype(BF16)
-    ends_in[me] = ends_out[lax.rem(me, 4)]
-    start_all(end_copy, n_ctx)
 
     for k in range(subs):
         at = slice(k * 8, (k + 1) * 8)
@@ -377,13 +385,6 @@
         )
         taps[c, 0:4, :] = 0.5 * tap[:, at]
         taps[c, 4:5, :] = 0.5 * move[:, at]
-
-    def project(block, ext):
-        here = pl.ds(pl.multiple_of(block * big, big), big)
-        for weights, first, count in ((value_ref, 0, 4), (state_ref, 4, 2)):
-            got = dot(rows_ref[here, :], weights[...])
-            for c in range(count):
-                ext[first + c, 8 : 8 + big, :] = got[:, c * 128 : (c + 1) * 128]
 
     def convolve(ext, c, at, length):
         h = taps[c, 4:5, :] + taps[c, 0:1, :] * ext[c, at + 5 : at + 5 + length, :]
@@ -416,10 +417,6 @@
             locs[k + 1] = factor * locs[k] + new
             fades[k + 1] = factor * fades[k]
 
-    def hand_on(source, ext):
-        for c in range(6):
-            ext[c, 0:8, :] = source[c, big : big + 8, :]
-
     def local(j, carry):
         advance(2 * j + 1, ext_a, ext_b, 2 * j + 2)
         hand_on(ext_a, ext_b)
@@ -427,9 +424,13 @@
         hand_on(ext_b, ext_a)
         return carry
 
-    project(0, ext_0)
-    project(1, ext_a)
-    hand_on(ext_0, ext_a)
+    pl.semaphore_wait(barrier, n_ctx - 1)
+    near_copy(1).start()
+    near_copy(2).start()
+
+    ends_in[me] = ends_out[lax.rem(me, 4)]
+    start_all(end_copy, n_ctx)
+
     lax.fori_loop(0, bigs // 2 - 1, local, 0)
 
     near_copy(1).wait()
@@ -469,12 +470,14 @@
     lower = iota((T, T), 1) <= iota((T, T), 0)
     left_half = iota((T, T), 1) < HEAD_DIM
 
+    wide = 4 * T
+
     def inside(i, carry):
-        g0 = pl.multiple_of(i * big, big)
-        here = pl.ds(g0, big)
+        g0 = pl.multiple_of(i * wide, wide)
+        here = pl.ds(g0, wide)
         parts = []
-        for q in range(big // T):
-            k = i * (big // T) + q
+        for q in range(wide // T):
+            k = i * (wide // T) + q
             at = pl.ds(pl.multiple_of(g0 + q * T, T), T)
             m = maps[at, :]
             scores = jnp.where(lower, dot_nt(m[:, STATE:], m[:, :STATE]), 0.0)
@@ -501,7 +504,7 @@
         open_gate[here, :] = silu(opened)
         return carry
 
-    half = bigs // 2
+    half = groups // wide // 2
     lax.fori_loop(0, half, inside, 0)
 
     wait_all(ends_in, end_send, ends_in, end_recv)
@@ -515,7 +518,7 @@
     ret_in[me] = ret_out[me]
     start_all(ret_copy, n_ctx)
 
-    lax.fori_loop(half, bigs, inside, 0)
+    lax.fori_loop(half, groups // wide, inside, 0)
 
     wait_all(ret_out, ret_send, ret_in, ret_recv)
     for k in range(n_ctx):

time: 55.8 us -> 54.1 us (0.970)
  Pallas kernels: 55.5 us -> 53.8 us
    pallas_call x1, Pallas kernels: 31.5 us -> 30.2 us  [layer(): pl.pallas_call(functools.partial(layer_kernel, n_ctx, groups), out_shape=...]
where the time goes in v5:
time: 54.1 us; the launch traced here: 54 us
  Pallas kernels  53.8 us (99%)
    pallas_call x1, Pallas kernels, layer(): pl.pallas_call(functools.partial(layer_kernel, n_ctx, groups), out_shape=...  30.2 us
    pallas_call x1, Pallas kernels, norm(): pl.pallas_call(functools.partial(norm_kernel, n_head, groups), out_shape=...  12.1 us
    pallas_call x1, Pallas kernels, compact(): pl.pallas_call(functools.partial(compact_kernel, groups), out_shape=[on_c...  7.63 us
    pallas_call x1, Pallas kernels, expand(): pl.pallas_call(functools.partial(expand_kernel, groups), out_shape=jax.Sh...  3.94 us

profile of v5, /device:TPU:1, one launch (start us, length us, event | category | flops | bytes accessed | tf_op | source)
XLA Modules:
  0.0 54.0 jit_solution(10455180499093588222)
XLA Ops:
  0.0 0.0 copy-start.1
  0.0 0.0 copy-start.2
  0.0 0.0 copy-start.3
  0.0 0.0 copy-start.4
  0.0 0.0 copy-start.5
  0.0 0.0 copy-start.6
  0.0 0.0 copy-start.7
  0.0 0.0 copy-start.8
  0.1 0.0 copy-start.9
  0.1 0.0 copy-start.10
  0.1 0.0 copy-start.11
  0.1 7.6 %shard_map.136 = (bf16[2320,2048]{1,0:T(8,128)(2,1)S(1)}, bf16[16,2048]{1,0:T(8,128)(2,1)S(1)}, s32[8,128]{1,0:T(8,128)S(1)}, f32[128,128]{1,0:T(8,128)S(1)}, s32[12]{0:T(128)S(1)}) custom-call(s32[3072]{0:T(1024)} %bnd_hbm.1, bf16[3072,2048]{1,0:T(8,128)(2,1)} %bytes_hbm.1), custom_call_target="tpu_custom_call" | custom-call | flops 3422552064 | bytes 12582912 | tf_op jit(solution)/shard_map/pallas_call | solution.py:162
  7.7 0.0 copy-done.1
  7.7 0.0 copy-done.2
  7.7 0.0 copy-done.3
  7.8 0.0 copy-done.4
  7.8 0.0 copy-done.5
  7.8 0.0 copy-done.6
  7.8 0.0 copy-done.7
  7.8 0.0 copy-done.8
  7.8 0.0 copy-done.9
  7.8 0.0 copy-done.10
  7.8 0.0 copy-done.11
  7.8 30.2 %shard_map.137 = (f32[2048,512]{1,0:T(8,128)S(1)}, f32[2048,512]{1,0:T(8,128)S(1)}, f32[16,128,512]{2,1,0:T(8,128)S(1)}, f32[17,128,512]{2,1,0:T(8,128)S(1)}, f3...) custom-call(bf16[2320,2048]{1,0:T(8,128)(2,1)S(1)} %get-tuple-elemen, ...), custom_call_target="tpu_custom_call" | custom-call | flops 12884901888 | bytes 8388608 | tf_op jit(solution)/shard_map/pallas_call | solution.py:668
  38.0 0.0 copy-start
  38.0 12.1 %shard_map.138 = (bf16[2176,512]{1,0:T(8,128)(2,1)S(1)}, f32[24,128]{1,0:T(8,128)S(1)}, bf16[3072,384]{1,0:T(8,128)(2,1)S(1)}) custom-call(f32[2048,512]{1,0:T(8,128)S(1)} %get-tuple-element.25.mix, f32[2048,512]{1,0:T(8,128)S(1)} %get-tuple-element.26.open_gate, f32[16,128,512]{2,1,0:T(8,128)S(1)} %get-tuple-element.27.grow, ...), custom_call_target="tpu_custom_call" | custom-call | flops 536870912 | bytes 1048576 | tf_op jit(solution)/shard_map/pallas_call | solution.py:638
  50.1 0.0 copy-done
  50.1 3.9 %shard_map.139 = f32[3072,512]{1,0:T(8,128)} custom-call(s32[12]{0:T(128)S(1)} %get-tuple-element.21.start_ref, bf16[3072,384]{1,0:T(8,128)(2,1)S(1)} %get-tuple-element.34.place_ref, bf16[2176,512]{1,0:T(8,128)(2,1)S(1)} %get-tuple-element.35.table_ref, f32[24,128]{1,0:T(8,128)S(1)} %get-tuple-element.36.inv_ref, f32[1,512]{1,0:T(1,128)S(1)} %bitcast.4), custom_call_target="tpu_custom_call" | custom-call | flops 1207959552 | bytes 6291456 | tf_op jit(solution)/shard_map/pallas_call | solution.py:758
Async XLA Ops:
  0.0 7.7 %copy-start.1 = (bf16[2048,512]{1,0:T(8,128)(2,1)S(1)}, bf16[2048,512]{1,0:T(8,128)(2,1)}, u32[]{:S(2)}) copy-start(bf16[2048,512]{1,0:T(8,128)(2,1)} %value_ref.1) | copy-start | bytes 6291460
  0.0 7.7 %copy-start.2 = (bf16[2048,512]{1,0:T(8,128)(2,1)S(1)}, bf16[2048,512]{1,0:T(8,128)(2,1)}, u32[]{:S(2)}) copy-start(bf16[2048,512]{1,0:T(8,128)(2,1)} %gate_ref.1) | copy-start | bytes 6291460
  0.0 7.7 %copy-start.3 = (bf16[2048,256]{1,0:T(8,128)(2,1)S(1)}, bf16[2048,256]{1,0:T(8,128)(2,1)}, u32[]{:S(2)}) copy-start(bf16[2048,256]{1,0:T(8,128)(2,1)} %state_ref.1) | copy-start | bytes 3145732
  0.0 7.8 %copy-start.4 = (bf16[2048,8]{0,1:T(8,128)(2,1)S(1)}, bf16[2048,8]{0,1:T(8,128)(2,1)}, u32[]{:S(2)}) copy-start(bf16[2048,8]{0,1:T(8,128)(2,1)} %param.19) | copy-start | bytes 98308
  0.0 7.8 %copy-start.5 = (f32[4,512]{1,0:T(4,128)S(1)}, f32[4,512]{1,0:T(4,128)}, u32[]{:S(2)}) copy-start(f32[4,512]{1,0:T(4,128)} %vconv_ref.1) | copy-start | bytes 24580
  0.0 7.8 %copy-start.6 = (f32[4,256]{1,0:T(4,128)S(1)}, f32[4,256]{1,0:T(4,128)}, u32[]{:S(2)}) copy-start(f32[4,256]{1,0:T(4,128)} %sconv_ref.1) | copy-start | bytes 12292
  0.0 7.8 %copy-start.7 = (f32[512]{0:T(512)S(1)}, f32[512]{0:T(512)}, u32[]{:S(2)}) copy-start(f32[512]{0:T(512)} %param.24) | copy-start | bytes 6148
  0.0 7.8 %copy-start.8 = (f32[256]{0:T(256)S(1)}, f32[256]{0:T(256)}, u32[]{:S(2)}) copy-start(f32[256]{0:T(256)} %param.26) | copy-start | bytes 3076
  0.1 7.8 %copy-start.9 = (f32[8]{0:T(128)S(1)}, f32[8]{0:T(128)}, u32[]{:S(2)}) copy-start(f32[8]{0:T(128)} %bias_ref.1) | copy-start | bytes 100
  0.1 7.8 %copy-start.10 = (f32[8]{0:T(128)S(1)}, f32[8]{0:T(128)}, u32[]{:S(2)}) copy-start(f32[8]{0:T(128)} %log_ref.1) | copy-start | bytes 100
  0.1 7.8 %copy-start.11 = (f32[8]{0:T(128)S(1)}, f32[8]{0:T(128)}, u32[]{:S(2)}) copy-start(f32[8]{0:T(128)} %skip_ref.1) | copy-start | bytes 100
  38.0 12.1 %copy-start = (f32[512]{0:T(512)S(1)}, f32[512]{0:T(512)}, u32[]{:S(2)}) copy-start(f32[512]{0:T(512)} %param.27) | copy-start | bytes 6148

commit v6 on v5

--- a/solution.py
+++ b/solution.py
@@ -18,7 +18,7 @@
 T = 128
 BLOCK = 256
 SPAN = BLOCK + 16
-UNROLL = 3
+UNROLL = 6
 JOINED = 1
 EPSILON = 1e-05
 LOG_FLOOR = -1e4
@@ -232,6 +232,7 @@
     ext_b,
     ext_h,
     taps,
+    factors,
     xs,
     raw_step,
     lead_t,
@@ -373,6 +374,14 @@
         lead_t[k] = jnp.concatenate([p[at] for p in cums] + [jnp.ones((24, T), F32)], 0).astype(BF16)
         lead_e[k] = jnp.concatenate([p[at] for p in grows + tails], 0).astype(BF16)
         minus[k] = jnp.concatenate([p[at] for p in lows], 0)
+    wide_shape = (subs * 8, WIDE)
+    own = iota(wide_shape, 0) % 8 == iota(wide_shape, 1) // HEAD_DIM
+    fade = jnp.where(own, jnp.concatenate([jnp.exp(total)] * 4, 1), 0.0)
+    which = flag(iota((subs, subs * 8), 1) // 8 == iota((subs, subs * 8), 0))
+    f0, f1 = pieces(fade, 2)
+    fade = dot(which, f0.astype(BF16)) + dot(which, f1.astype(BF16))
+    for k in range(subs):
+        factors[k] = fade[k : k + 1, :]
     head_of = iota((24, 8 * T), 0) % 8
     sel_d[...] = flag(head_of == iota((24, 8 * T), 1) // T).astype(F32)
     row, lane = iota((32, 2 * WIDE), 0), iota((32, 2 * WIDE), 1)
@@ -397,23 +406,22 @@
         fades[k] = jnp.ones((1, WIDE), F32)
 
     def advance(block, ext, onto, target):
-        both = [dot_tn(lead_e[block * 2 + q], sel_e[...]) for q in range(2)]
+        tails = [dot_tn(lead_e[block * 2 + q], sel_e[:, WIDE:]) for q in range(2)]
         if target is not None:
             project(target, onto)
         for q in range(2):
             k = block * 2 + q
             at = pl.ds(pl.multiple_of(k * T, T), T)
-            grow[k] = both[q][:, :WIDE]
             weighted = []
             for c in range(4):
                 x = convolve(ext, c, q * T, T)
                 xs[at, c * 128 : (c + 1) * 128] = x.astype(BF16)
-                tail = both[q][:, WIDE + c * 128 : WIDE + (c + 1) * 128]
+                tail = tails[q][:, c * 128 : (c + 1) * 128]
                 weighted.append((x * tail).astype(BF16))
             for c in range(2):
                 maps[at, c * 128 : (c + 1) * 128] = convolve(ext, 4 + c, q * T, T).astype(BF16)
             new = dot_tn(maps[at, :STATE], jnp.concatenate(weighted, 1))
-            factor = both[q][T - 1 : T, :WIDE]
+            factor = factors[k]
             locs[k + 1] = factor * locs[k] + new
             fades[k + 1] = factor * fades[k]
 
@@ -470,7 +478,7 @@
     lower = iota((T, T), 1) <= iota((T, T), 0)
     left_half = iota((T, T), 1) < HEAD_DIM
 
-    wide = 4 * T
+    wide = min(8 * T, groups // 2)
 
     def inside(i, carry):
         g0 = pl.multiple_of(i * wide, wide)
@@ -479,6 +487,7 @@
         for q in range(wide // T):
             k = i * (wide // T) + q
             at = pl.ds(pl.multiple_of(g0 + q * T, T), T)
+            grow[k] = dot_tn(lead_e[k], sel_e[:, :WIDE])
             m = maps[at, :]
             scores = jnp.where(lower, dot_nt(m[:, STATE:], m[:, :STATE]), 0.0)
             tile = jnp.concatenate([minus[k]] * HEADS_HERE, 1) * sel_d[...]
@@ -685,6 +694,7 @@
             pltpu.VMEM((6, 2 * T + 8, 128), F32),
             pltpu.VMEM((6, 24, 128), F32),
             pltpu.VMEM((6, 8, 128), F32),
+            pltpu.VMEM((subs, 1, WIDE), F32),
             pltpu.VMEM((groups, WIDE), BF16),
             pltpu.VMEM((subs * 8, T), F32),
             pltpu.VMEM((subs, 48, T), BF16),
@@ -745,6 +755,8 @@
         return carry
 
     lax.fori_loop(0, blocks // UNROLL, steps, 0)
+    for j in range(blocks - blocks % UNROLL, blocks):
+        step(j, 0)
 
     def finish(j, carry):
         send(j).wait()

time: 54.1 us -> 53.6 us (level)
  Pallas kernels: 53.8 us -> 53.1 us
    pallas_call x1, Pallas kernels: 30.2 us -> 29.4 us  [layer(): pl.pallas_call(functools.partial(layer_kernel, n_ctx, groups), out_shape=...]
where the time goes in v6:
time: 53.6 us
  Pallas kernels  53.1 us (99%)
    pallas_call x1, Pallas kernels, layer(): pl.pallas_call(functools.partial(layer_kernel, n_ctx, groups), out_shape=...  29.4 us
    pallas_call x1, Pallas kernels, norm(): pl.pallas_call(functools.partial(norm_kernel, n_head, groups), out_shape=...  12.1 us
    pallas_call x1, Pallas kernels, compact(): pl.pallas_call(functools.partial(compact_kernel, groups), out_shape=[on_c...  8.02 us
    pallas_call x1, Pallas kernels, expand(): pl.pallas_call(functools.partial(expand_kernel, groups), out_shape=jax.Sh...  3.65 us

profile of v6, /device:TPU:1, one launch (start us, length us, event | category | flops | bytes accessed | tf_op | source)
XLA Modules:
  0.0 53.6 jit_solution(1953743744181877361)
XLA Ops:
  0.0 0.0 copy-start.1
  0.0 0.0 copy-start.2
  0.0 0.0 copy-start.3
  0.0 0.0 copy-start.4
  0.0 0.0 copy-start.5
  0.0 0.0 copy-start.6
  0.0 0.0 copy-start.7
  0.0 0.0 copy-start.8
  0.1 0.0 copy-start.9
  0.1 0.0 copy-start.10
  0.1 0.0 copy-start.11
  0.1 8.0 %shard_map.136 = (bf16[2320,2048]{1,0:T(8,128)(2,1)S(1)}, bf16[16,2048]{1,0:T(8,128)(2,1)S(1)}, s32[8,128]{1,0:T(8,128)S(1)}, f32[128,128]{1,0:T(8,128)S(1)}, s32[12]{0:T(128)S(1)}) custom-call(s32[3072]{0:T(1024)} %bnd_hbm.1, bf16[3072,2048]{1,0:T(8,128)(2,1)} %bytes_hbm.1), custom_call_target="tpu_custom_call" | custom-call | flops 3422552064 | bytes 12582912 | tf_op jit(solution)/shard_map/pallas_call | solution.py:162
  8.1 0.0 copy-done.1
  8.1 0.0 copy-done.2
  8.1 0.0 copy-done.3
  8.1 0.0 copy-done.4
  8.2 0.0 copy-done.5
  8.2 0.0 copy-done.6
  8.2 0.0 copy-done.7
  8.2 0.0 copy-done.8
  8.2 0.0 copy-done.9
  8.2 0.0 copy-done.10
  8.2 0.0 copy-done.11
  8.2 29.4 %shard_map.137 = (f32[2048,512]{1,0:T(8,128)S(1)}, f32[2048,512]{1,0:T(8,128)S(1)}, f32[16,128,512]{2,1,0:T(8,128)S(1)}, f32[17,128,512]{2,1,0:T(8,128)S(1)}, f3...) custom-call(bf16[2320,2048]{1,0:T(8,128)(2,1)S(1)} %get-tuple-elemen, ...), custom_call_target="tpu_custom_call" | custom-call | flops 12884901888 | bytes 8388608 | tf_op jit(solution)/shard_map/pallas_call | solution.py:677
  37.6 0.0 copy-start
  37.7 12.1 %shard_map.138 = (bf16[2176,512]{1,0:T(8,128)(2,1)S(1)}, f32[24,128]{1,0:T(8,128)S(1)}, bf16[3072,384]{1,0:T(8,128)(2,1)S(1)}) custom-call(f32[2048,512]{1,0:T(8,128)S(1)} %get-tuple-element.25.mix, f32[2048,512]{1,0:T(8,128)S(1)} %get-tuple-element.26.open_gate, f32[16,128,512]{2,1,0:T(8,128)S(1)} %get-tuple-element.27.grow, ...), custom_call_target="tpu_custom_call" | custom-call | flops 536870912 | bytes 1048576 | tf_op jit(solution)/shard_map/pallas_call | solution.py:647
  49.7 0.0 copy-done
  49.7 3.6 %shard_map.139 = f32[3072,512]{1,0:T(8,128)} custom-call(s32[12]{0:T(128)S(1)} %get-tuple-element.21.start_ref, bf16[3072,384]{1,0:T(8,128)(2,1)S(1)} %get-tuple-element.34.place_ref, bf16[2176,512]{1,0:T(8,128)(2,1)S(1)} %get-tuple-element.35.table_ref, f32[24,128]{1,0:T(8,128)S(1)} %get-tuple-element.36.inv_ref, f32[1,512]{1,0:T(1,128)S(1)} %bitcast.4), custom_call_target="tpu_custom_call" | custom-call | flops 1207959552 | bytes 6291456 | tf_op jit(solution)/shard_map/pallas_call | solution.py:770
Async XLA Ops:
  0.0 8.1 %copy-start.1 = (bf16[2048,512]{1,0:T(8,128)(2,1)S(1)}, bf16[2048,512]{1,0:T(8,128)(2,1)}, u32[]{:S(2)}) copy-start(bf16[2048,512]{1,0:T(8,128)(2,1)} %value_ref.1) | copy-start | bytes 6291460
  0.0 8.1 %copy-start.2 = (bf16[2048,512]{1,0:T(8,128)(2,1)S(1)}, bf16[2048,512]{1,0:T(8,128)(2,1)}, u32[]{:S(2)}) copy-start(bf16[2048,512]{1,0:T(8,128)(2,1)} %gate_ref.1) | copy-start | bytes 6291460
  0.0 8.1 %copy-start.3 = (bf16[2048,256]{1,0:T(8,128)(2,1)S(1)}, bf16[2048,256]{1,0:T(8,128)(2,1)}, u32[]{:S(2)}) copy-start(bf16[2048,256]{1,0:T(8,128)(2,1)} %state_ref.1) | copy-start | bytes 3145732
  0.0 8.1 %copy-start.4 = (bf16[2048,8]{0,1:T(8,128)(2,1)S(1)}, bf16[2048,8]{0,1:T(8,128)(2,1)}, u32[]{:S(2)}) copy-start(bf16[2048,8]{0,1:T(8,128)(2,1)} %param.19) | copy-start | bytes 98308
  0.0 8.1 %copy-start.5 = (f32[4,512]{1,0:T(4,128)S(1)}, f32[4,512]{1,0:T(4,128)}, u32[]{:S(2)}) copy-start(f32[4,512]{1,0:T(4,128)} %vconv_ref.1) | copy-start | bytes 24580
  0.0 8.1 %copy-start.6 = (f32[4,256]{1,0:T(4,128)S(1)}, f32[4,256]{1,0:T(4,128)}, u32[]{:S(2)}) copy-start(f32[4,256]{1,0:T(4,128)} %sconv_ref.1) | copy-start | bytes 12292
  0.0 8.1 %copy-start.7 = (f32[512]{0:T(512)S(1)}, f32[512]{0:T(512)}, u32[]{:S(2)}) copy-start(f32[512]{0:T(512)} %param.24) | copy-start | bytes 6148
  0.0 8.1 %copy-start.8 = (f32[256]{0:T(256)S(1)}, f32[256]{0:T(256)}, u32[]{:S(2)}) copy-start(f32[256]{0:T(256)} %param.26) | copy-start | bytes 3076
  0.1 8.1 %copy-start.9 = (f32[8]{0:T(128)S(1)}, f32[8]{0:T(128)}, u32[]{:S(2)}) copy-start(f32[8]{0:T(128)} %bias_ref.1) | copy-start | bytes 100
  0.1 8.1 %copy-start.10 = (f32[8]{0:T(128)S(1)}, f32[8]{0:T(128)}, u32[]{:S(2)}) copy-start(f32[8]{0:T(128)} %log_ref.1) | copy-start | bytes 100
  0.1 8.1 %copy-start.11 = (f32[8]{0:T(128)S(1)}, f32[8]{0:T(128)}, u32[]{:S(2)}) copy-start(f32[8]{0:T(128)} %skip_ref.1) | copy-start | bytes 100
  37.6 12.1 %copy-start = (f32[512]{0:T(512)S(1)}, f32[512]{0:T(512)}, u32[]{:S(2)}) copy-start(f32[512]{0:T(512)} %param.27) | copy-start | bytes 6148

commit v7 on v6

--- a/solution.py
+++ b/solution.py
@@ -600,9 +600,11 @@
     mine[...] = jnp.zeros(mine.shape, F32)
     mine[0:1, :] = dot_nt(ones, power)[0:1, :]
 
+    together = min(8, subs)
+
     def outer(i, carry):
-        for q in range(4):
-            k = i * 4 + q
+        for q in range(together):
+            k = i * together + q
             at = pl.ds(pl.multiple_of(k * T, T), T)
             state = (locs[k] + fades[k] * base[jnp.where(k > 2, 1, 0)]).astype(BF16)
             gated = mix[at, :] + grow[k] * dot(maps[at, STATE:], state)
@@ -611,7 +613,7 @@
             squares[column, pl.ds(k + 1, 1), :] = dot_nt(ones, (gated * gated).astype(BF16))[0:1, :]
         return carry
 
-    lax.fori_loop(0, subs // 4, outer, 0)
+    lax.fori_loop(0, subs // together, outer, 0)
 
     pl.semaphore_wait(barrier, n_head - 1)
     start_all(sq_copy, n_head)

time: 53.6 us -> 53.1 us (level)
  Pallas kernels: 53.1 us -> 52.5 us
    pallas_call x1, Pallas kernels: 29.4 us -> 28.9 us  [layer(): pl.pallas_call(functools.partial(layer_kernel, n_ctx, groups), out_shape=...]
where the time goes in v7:
time: 53.1 us; the launch traced here: 52.9 us
  Pallas kernels  52.5 us (99%)
    pallas_call x1, Pallas kernels, layer(): pl.pallas_call(functools.partial(layer_kernel, n_ctx, groups), out_shape=...  28.9 us
    pallas_call x1, Pallas kernels, norm(): pl.pallas_call(functools.partial(norm_kernel, n_head, groups), out_shape=...  11.6 us
    pallas_call x1, Pallas kernels, compact(): pl.pallas_call(functools.partial(compact_kernel, groups), out_shape=[on_c...  8.37 us
    pallas_call x1, Pallas kernels, expand(): pl.pallas_call(functools.partial(expand_kernel, groups), out_shape=jax.Sh...  3.64 us

profile of v7, /device:TPU:1, one launch (start us, length us, event | category | flops | bytes accessed | tf_op | source)
XLA Modules:
  0.0 52.9 jit_solution(8736998029543734998)
XLA Ops:
  0.0 0.0 copy-start.1
  0.0 0.0 copy-start.2
  0.0 0.0 copy-start.3
  0.0 0.0 copy-start.4
  0.0 0.0 copy-start.5
  0.0 0.0 copy-start.6
  0.0 0.0 copy-start.7
  0.0 0.0 copy-start.8
  0.1 0.0 copy-start.9
  0.1 0.0 copy-start.10
  0.1 0.0 copy-start.11
  0.1 8.4 %shard_map.136 = (bf16[2320,2048]{1,0:T(8,128)(2,1)S(1)}, bf16[16,2048]{1,0:T(8,128)(2,1)S(1)}, s32[8,128]{1,0:T(8,128)S(1)}, f32[128,128]{1,0:T(8,128)S(1)}, s32[12]{0:T(128)S(1)}) custom-call(s32[3072]{0:T(1024)} %bnd_hbm.1, bf16[3072,2048]{1,0:T(8,128)(2,1)} %bytes_hbm.1), custom_call_target="tpu_custom_call" | custom-call | flops 3422552064 | bytes 12582912 | tf_op jit(solution)/shard_map/pallas_call | solution.py:162
  8.5 0.0 copy-done.1
  8.5 0.0 copy-done.2
  8.5 0.0 copy-done.3
  8.5 0.0 copy-done.4
  8.5 0.0 copy-done.5
  8.5 0.0 copy-done.6
  8.5 0.0 copy-done.7
  8.5 0.0 copy-done.8
  8.5 0.0 copy-done.9
  8.6 0.0 copy-done.10
  8.6 0.0 copy-done.11
  8.6 28.9 %shard_map.137 = (f32[2048,512]{1,0:T(8,128)S(1)}, f32[2048,512]{1,0:T(8,128)S(1)}, f32[16,128,512]{2,1,0:T(8,128)S(1)}, f32[17,128,512]{2,1,0:T(8,128)S(1)}, f3...) custom-call(bf16[2320,2048]{1,0:T(8,128)(2,1)S(1)} %get-tuple-elemen, ...), custom_call_target="tpu_custom_call" | custom-call | flops 12884901888 | bytes 8388608 | tf_op jit(solution)/shard_map/pallas_call | solution.py:679
  37.5 0.0 copy-start
  37.5 11.6 %shard_map.138 = (bf16[2176,512]{1,0:T(8,128)(2,1)S(1)}, f32[24,128]{1,0:T(8,128)S(1)}, bf16[3072,384]{1,0:T(8,128)(2,1)S(1)}) custom-call(f32[2048,512]{1,0:T(8,128)S(1)} %get-tuple-element.25.mix, f32[2048,512]{1,0:T(8,128)S(1)} %get-tuple-element.26.open_gate, f32[16,128,512]{2,1,0:T(8,128)S(1)} %get-tuple-element.27.grow, ...), custom_call_target="tpu_custom_call" | custom-call | flops 536870912 | bytes 1048576 | tf_op jit(solution)/shard_map/pallas_call | solution.py:649
  49.1 0.0 copy-done
  49.1 3.6 %shard_map.139 = f32[3072,512]{1,0:T(8,128)} custom-call(s32[12]{0:T(128)S(1)} %get-tuple-element.21.start_ref, bf16[3072,384]{1,0:T(8,128)(2,1)S(1)} %get-tuple-element.34.place_ref, bf16[2176,512]{1,0:T(8,128)(2,1)S(1)} %get-tuple-element.35.table_ref, f32[24,128]{1,0:T(8,128)S(1)} %get-tuple-element.36.inv_ref, f32[1,512]{1,0:T(1,128)S(1)} %bitcast.4), custom_call_target="tpu_custom_call" | custom-call | flops 1207959552 | bytes 6291456 | tf_op jit(solution)/shard_map/pallas_call | solution.py:772
Async XLA Ops:
  0.0 8.5 %copy-start.1 = (bf16[2048,512]{1,0:T(8,128)(2,1)S(1)}, bf16[2048,512]{1,0:T(8,128)(2,1)}, u32[]{:S(2)}) copy-start(bf16[2048,512]{1,0:T(8,128)(2,1)} %value_ref.1) | copy-start | bytes 6291460
  0.0 8.5 %copy-start.2 = (bf16[2048,512]{1,0:T(8,128)(2,1)S(1)}, bf16[2048,512]{1,0:T(8,128)(2,1)}, u32[]{:S(2)}) copy-start(bf16[2048,512]{1,0:T(8,128)(2,1)} %gate_ref.1) | copy-start | bytes 6291460
  0.0 8.5 %copy-start.3 = (bf16[2048,256]{1,0:T(8,128)(2,1)S(1)}, bf16[2048,256]{1,0:T(8,128)(2,1)}, u32[]{:S(2)}) copy-start(bf16[2048,256]{1,0:T(8,128)(2,1)} %state_ref.1) | copy-start | bytes 3145732
  0.0 8.5 %copy-start.4 = (bf16[2048,8]{0,1:T(8,128)(2,1)S(1)}, bf16[2048,8]{0,1:T(8,128)(2,1)}, u32[]{:S(2)}) copy-start(bf16[2048,8]{0,1:T(8,128)(2,1)} %param.19) | copy-start | bytes 98308
  0.0 8.5 %copy-start.5 = (f32[4,512]{1,0:T(4,128)S(1)}, f32[4,512]{1,0:T(4,128)}, u32[]{:S(2)}) copy-start(f32[4,512]{1,0:T(4,128)} %vconv_ref.1) | copy-start | bytes 24580
  0.0 8.5 %copy-start.6 = (f32[4,256]{1,0:T(4,128)S(1)}, f32[4,256]{1,0:T(4,128)}, u32[]{:S(2)}) copy-start(f32[4,256]{1,0:T(4,128)} %sconv_ref.1) | copy-start | bytes 12292
  0.0 8.5 %copy-start.7 = (f32[512]{0:T(512)S(1)}, f32[512]{0:T(512)}, u32[]{:S(2)}) copy-start(f32[512]{0:T(512)} %param.24) | copy-start | bytes 6148
  0.0 8.5 %copy-start.8 = (f32[256]{0:T(256)S(1)}, f32[256]{0:T(256)}, u32[]{:S(2)}) copy-start(f32[256]{0:T(256)} %param.26) | copy-start | bytes 3076
  0.1 8.5 %copy-start.9 = (f32[8]{0:T(128)S(1)}, f32[8]{0:T(128)}, u32[]{:S(2)}) copy-start(f32[8]{0:T(128)} %bias_ref.1) | copy-start | bytes 100
  0.1 8.5 %copy-start.10 = (f32[8]{0:T(128)S(1)}, f32[8]{0:T(128)}, u32[]{:S(2)}) copy-start(f32[8]{0:T(128)} %log_ref.1) | copy-start | bytes 100
  0.1 8.5 %copy-start.11 = (f32[8]{0:T(128)S(1)}, f32[8]{0:T(128)}, u32[]{:S(2)}) copy-start(f32[8]{0:T(128)} %skip_ref.1) | copy-start | bytes 100
  37.5 11.6 %copy-start = (f32[512]{0:T(512)S(1)}, f32[512]{0:T(512)}, u32[]{:S(2)}) copy-start(f32[512]{0:T(512)} %param.27) | copy-start | bytes 6148
